TPU v7x, 32 devices: a whole 2x2x4 slice. The times are simulated.
32 devices in a mesh: gz: 4 (over x, core), gx: 8 (over z, y).
Axes of the slice: x: 2, y: 2, z: 4, core: 2. Of those that a mesh axis runs over, the one named last changes fastest.
Arguments:
- state: float32 [6, 64, 2048], P(None, 'gz', 'gx'), may hold values from -5 to 5, as said below
- state_cot: float32 [6, 64, 2048], P(None, 'gz', 'gx'), may hold values from -6 to 6
- w_in: bfloat16 [128, 12], replicated, may hold values from -1.75 to 1.75
- w_mid: bfloat16 [128, 128], replicated, may hold values from -0.5 to 0.5
- w_out: bfloat16 [6, 128], replicated, may hold values from -0.5 to 0.5
- radiation: float32 [64, 64], replicated, may hold values from -0.75 to 0.75
- fall_rate: float32 [2048], P('gx'), may hold values from 20 to 2000
- active: int32 [2048], P('gx'), may hold values 0 or 1
Outputs:
- new_state: float32 [6, 64, 2048], P(None, 'gz', 'gx')
- state_grad: float32 [6, 64, 2048], P(None, 'gz', 'gx')
- grad_in: float32 [128, 12], replicated
- grad_mid: float32 [128, 128], replicated
- grad_out: float32 [6, 128], replicated
Inputs may be any that keep to these rules, and one draw needn't show every extreme that they name: `state`: fields come in the order u, v, w, theta, total water, rain water; rain water lies between 0.05 and 1.
All inputs are finite; a program needn't handle non-finite values. No bound on the sum of `active` on one device may be relied on, other than what follows from the above.
Results may differ from a plain program's by a relative error of at most 0.00045.
The roundings to bfloat16 on the way count: a program that leaves them out, or rounds other values in their place, can miss the bound.
Values sent between devices are 32-bit elements; how exact they have to be, the bound alone decides.
A program may use at most 64 MiB of HBM per device.

v0:
```python
import jax
import jax.numpy as jnp
from jax import lax
from jax.sharding import PartitionSpec as P

NY = 64


DIFFUSION = 0.1
TIME_STEP = 0.25
CLOSURE_GAIN = 1.0
HEATING_GAIN = 1.0
FALL_GAIN = 1.0


def prefix(shard, axis, combine, identity, reverse):
    length, index = (lax.axis_size(axis), lax.axis_index(axis))
    everything = jax.tree.map(lambda part: lax.all_gather(part, axis), shard)
    start = jax.tree.map(
        lambda part, zero: jnp.broadcast_to(jnp.asarray(zero, part.dtype), part.shape),
        shard,
        identity,
    )

    def step(k, before):
        at = length - 1 - k if reverse else k
        reached = at > index if reverse else at < index
        new = combine(before, jax.tree.map(lambda part: part[at], everything))
        return jax.tree.map(lambda a, b: jnp.where(reached, a, b), new, before)

    return lax.fori_loop(0, length, step, start)


def passed_along(shard, axis, by):
    length = lax.axis_size(axis)
    return lax.ppermute(shard, axis, [(i, (i + by) % length) for i in range(length)])


def padded_2(shard, sides, width):
    for axis, dim in sides:
        size, length = (lax.axis_size(axis), shard.shape[dim])
        up = [(i, (i + 1) % size) for i in range(size)]
        down = [(j, i) for i, j in up]
        last = lax.slice_in_dim(shard, length - width, length, axis=dim)
        first = lax.slice_in_dim(shard, 0, width, axis=dim)
        before = lax.ppermute(last, axis, up)
        after = lax.ppermute(first, axis, down)
        shard = jnp.concatenate([before, shard, after], axis=dim)
    return shard


def contract(left, right, left_dim, right_dim):
    return lax.dot_general(
        left, right, (((left_dim,), (right_dim,)), ((), ())), preferred_element_type=jnp.float32
    )


def mlp_forward(features, w_in, w_mid, w_out):
    hidden_one = jnp.tanh(jnp.dot(w_in, features, preferred_element_type=jnp.float32)).astype(
        jnp.bfloat16
    )
    hidden_two = jnp.tanh(jnp.dot(w_mid, hidden_one, preferred_element_type=jnp.float32)).astype(
        jnp.bfloat16
    )
    return jnp.dot(w_out, hidden_two, preferred_element_type=jnp.float32)


def mlp_backward(features, out_cot, w_in, w_mid, w_out):
    tanh_one = jnp.tanh(jnp.dot(w_in, features, preferred_element_type=jnp.float32))
    hidden_one = tanh_one.astype(jnp.bfloat16)
    tanh_two = jnp.tanh(jnp.dot(w_mid, hidden_one, preferred_element_type=jnp.float32))
    hidden_two = tanh_two.astype(jnp.bfloat16)
    term_out = contract(out_cot, hidden_two, 1, 1)
    pre_two = (contract(w_out, out_cot, 0, 0) * (1.0 - tanh_two * tanh_two)).astype(jnp.bfloat16)
    term_mid = contract(pre_two, hidden_one, 1, 1)
    pre_one = (contract(w_mid, pre_two, 0, 0) * (1.0 - tanh_one * tanh_one)).astype(jnp.bfloat16)
    term_in = contract(pre_one, features, 1, 1)
    feature_cot = contract(w_in, pre_one, 0, 0)
    return (feature_cot, (term_in, term_mid, term_out))


def interior(padded):
    return padded[..., 2 * NY : padded.shape[-1] - 2 * NY]


def dynamics(padded):
    columns = padded.shape[-1] - 4 * NY

    def along_x(offset):
        first_col = 2 * NY + offset * NY
        return padded[..., first_col : first_col + columns]

    center = along_x(0)
    y_place = jnp.arange(columns) % NY
    y_last = y_place == NY - 1
    y_first = y_place == 0
    y_plus = jnp.where(y_last, jnp.roll(center, NY - 1, -1), jnp.roll(center, -1, -1))
    y_minus = jnp.where(y_first, jnp.roll(center, 1 - NY, -1), jnp.roll(center, 1, -1))
    x_plus, x_minus = (along_x(1), along_x(-1))
    deriv_x = (8.0 * (x_plus - x_minus) - (along_x(2) - along_x(-2))) / 12.0
    deriv_y = (y_plus - y_minus) / 2.0
    laplace = x_plus + x_minus + y_plus + y_minus - 4.0 * center
    return (-(center[0] * deriv_x + center[1] * deriv_y) + DIFFUSION * laplace, deriv_x)


def compose(earlier, later):
    return (later[0] * earlier[0], later[1] + later[0] * earlier[1])


def running_maps(source, retained):
    factors = jnp.broadcast_to(retained, source.shape)
    return lax.associative_scan(compose, (factors, source), axis=0)


def sediment_forward(rain_water, fall_speed):
    fresh_share = 1.0 / (1.0 + fall_speed)
    retained = fall_speed / (1.0 + fall_speed)
    factors, values = running_maps(jnp.flip(fresh_share * rain_water, 0), retained)
    inflow = prefix(
        (factors[-1], values[-1]),
        "gz",
        compose,
        (jnp.ones_like(fall_speed), jnp.zeros_like(fall_speed)),
        True,
    )
    return jnp.flip(values + factors * inflow[1], 0)


def sediment_adjoint(source, fall_speed):
    fresh_share = 1.0 / (1.0 + fall_speed)
    retained = fall_speed / (1.0 + fall_speed)
    factors, values = running_maps(fresh_share * source, retained)
    inflow = prefix(
        (factors[-1], values[-1]),
        "gz",
        compose,
        (jnp.ones_like(fall_speed), jnp.zeros_like(fall_speed)),
        False,
    )
    return values + factors * inflow[1]


def heating(theta, radiation):
    levels = theta.shape[0]
    own_rows = lax.dynamic_slice_in_dim(radiation, lax.axis_index("gz") * levels, levels, 0)
    return jnp.dot(
        own_rows,
        lax.all_gather(theta, "gz", axis=0, tiled=True),
        precision=lax.Precision.HIGHEST,
        preferred_element_type=jnp.float32,
    )


def heating_adjoint(lead_theta, radiation):
    levels = lead_theta.shape[0]
    own_rows = lax.dynamic_slice_in_dim(radiation, lax.axis_index("gz") * levels, levels, 0)
    return lax.psum_scatter(
        lax.dot_general(
            own_rows,
            lead_theta,
            (((0,), (0,)), ((), ())),
            precision=lax.Precision.HIGHEST,
            preferred_element_type=jnp.float32,
        ),
        "gz",
        scatter_dimension=0,
        tiled=True,
    )


def tendency(padded, w_in, w_mid, w_out, radiation, fall_speed, live):
    moved, deriv_x = dynamics(padded)
    center = interior(padded)
    fields, levels, columns = center.shape
    features = (
        jnp.concatenate([center, deriv_x], 0)
        .astype(jnp.bfloat16)
        .reshape(2 * fields, levels * columns)
    )
    closure = mlp_forward(features, w_in, w_mid, w_out).reshape(fields, levels, columns)
    total = moved + CLOSURE_GAIN * closure
    total = total.at[3].add(HEATING_GAIN * heating(center[3], radiation))
    fallen = sediment_forward(center[5], fall_speed)
    return total.at[5].add(FALL_GAIN * live * (fallen - center[5]))


def adjoint_tendency(padded, lead, w_in, w_mid, w_out, radiation, fall_speed, live):
    outputs, pullback = jax.vjp(dynamics, padded)
    center = interior(padded)
    fields, levels, columns = center.shape
    features = (
        jnp.concatenate([center, outputs[1]], 0)
        .astype(jnp.bfloat16)
        .reshape(2 * fields, levels * columns)
    )
    out_cot = (CLOSURE_GAIN * lead).astype(jnp.bfloat16).reshape(fields, levels * columns)
    feature_cot, grads = mlp_backward(features, out_cot, w_in, w_mid, w_out)
    feature_cot = feature_cot.reshape(2 * fields, levels, columns)
    padded_cot = pullback((lead, feature_cot[fields:]))[0]
    rim_width = 2 * NY
    from_next = passed_along(padded_cot[..., :rim_width], "gx", -1)
    from_prev = passed_along(padded_cot[..., padded_cot.shape[-1] - rim_width :], "gx", 1)
    result = interior(padded_cot) + feature_cot[:fields]
    result = result.at[..., :rim_width].add(from_prev)
    result = result.at[..., columns - rim_width :].add(from_next)
    result = result.at[3].add(HEATING_GAIN * heating_adjoint(lead[3], radiation))
    masked = live * lead[5]
    return (result.at[5].add(FALL_GAIN * (sediment_adjoint(masked, fall_speed) - masked)), grads)


def on_device(state, state_cot, w_in, w_mid, w_out, radiation, fall_rate, active):
    live = active.astype(jnp.float32)

    def extend(fields):
        return padded_2(fields, (("gx", 2),), 2 * NY)

    def section_tendency(padded):
        return tendency(padded, w_in, w_mid, w_out, radiation, fall_rate, live)

    def section_adjoint(padded, lead):
        return adjoint_tendency(padded, lead, w_in, w_mid, w_out, radiation, fall_rate, live)

    padded_zero = extend(state)
    section_one = state + TIME_STEP * section_tendency(padded_zero)
    padded_one = extend(section_one)
    section_two = 0.75 * state + 0.25 * (section_one + TIME_STEP * section_tendency(padded_one))
    padded_two = extend(section_two)
    new_state = state / 3.0 + 2.0 / 3.0 * (section_two + TIME_STEP * section_tendency(padded_two))
    lead_two = 2.0 / 3.0 * state_cot
    grad_state = state_cot / 3.0
    back_two, grads_two = section_adjoint(padded_two, lead_two)
    cot_two = lead_two + TIME_STEP * back_two
    lead_one = 0.25 * cot_two
    grad_state = grad_state + 0.75 * cot_two
    back_one, grads_one = section_adjoint(padded_one, lead_one)
    cot_one = lead_one + TIME_STEP * back_one
    back_zero, grads_zero = section_adjoint(padded_zero, cot_one)
    grad_state = grad_state + cot_one + TIME_STEP * back_zero
    totals = lax.psum(
        (
            TIME_STEP * (grads_two[0] + grads_one[0] + grads_zero[0]),
            TIME_STEP * (grads_two[1] + grads_one[1] + grads_zero[1]),
            TIME_STEP * (grads_two[2] + grads_one[2] + grads_zero[2]),
        ),
        ("gz", "gx"),
    )
    return (new_state, grad_state, totals[0], totals[1], totals[2])


def solution(mesh):
    placed = (P(None, "gz", "gx"), P(None, "gz", "gx"), P(), P(), P(), P(), P("gx"), P("gx"))
    return jax.shard_map(
        on_device,
        mesh=mesh,
        in_specs=placed,
        out_specs=(P(None, "gz", "gx"), P(None, "gz", "gx"), P(), P(), P()),
        check_vma=False,
    )
```

profile of v0, /device:TPU:0, one launch (start us, length us, event | category | flops | bytes accessed | tf_op | source)
XLA Modules:
  0.0 361.8 jit_solution(4317153807722568707)
XLA Ops:
  8.1 6.1 %collective-permute-start = (f32[6,16,128]{2,1,0:T(8,128)S(1)}, f32[6,16,128]{2,1,0:T(8,128)S(1)}, u32[]{:S(2)}, u32[]{:S(2)}) collective-permute-start(f32[6,16,128]{2,1,0:T(8,128)S(1)} %get-tuple-element.1230), channel_id=1, source_target_pairs={{1,0},{2,1},{3,2},{4,3},{5,4},{6,5},{7,6},{0,7},{9,8},{10,9},{11,1... | collective-permute-start | bytes 147464 | tf_op jit(solution)/shard_map/ppermute | solution.py:47
  20.5 5.1 %all-gather.3 = f32[4,1,256]{2,1,0:T(1,128)S(1)} all-gather(f32[1,1,256]{2,1,0:T(1,128)S(1)} %add_bitcast_fusion.6), channel_id=1, replica_groups=mesh['gz'=4,'gx'=8] {'gz'}, dimensions={0}, use_global_device_ids=true | all-gather | bytes 5120 | tf_op jit(solution)/shard_map/all_gather | solution.py:18
  25.5 5.1 %all-gather.4 = f32[4,1,256]{2,1,0:T(1,128)S(1)} all-gather(f32[1,1,256]{2,1,0:T(1,128)S(1)} %add_bitcast_fusion.5), channel_id=1, replica_groups=mesh['gz'=4,'gx'=8] {'gz'}, dimensions={0}, use_global_device_ids=true | all-gather | bytes 5120 | tf_op jit(solution)/shard_map/all_gather | solution.py:18
  31.1 5.2 %all-gather = f32[1,64,256]{2,1,0:T(8,128)S(1)} all-gather(f32[1,16,256]{2,1,0:T(8,128)S(1)} %slice-done), channel_id=2, replica_groups=mesh['gz'=4,'gx'=8] {'gz'}, dimensions={1}, use_global_device_ids=true | all-gather | bytes 81920 | tf_op jit(solution)/shard_map/all_gather | solution.py:148
  43.0 5.1 %all-gather.5 = f32[4,1,256]{2,1,0:T(1,128)S(1)} all-gather(f32[1,1,256]{2,1,0:T(1,128)S(1)} %add_bitcast_fusion.4), channel_id=1, replica_groups=mesh['gz'=4,'gx'=8] {'gz'}, dimensions={0}, use_global_device_ids=true | all-gather | bytes 5120 | tf_op jit(solution)/shard_map/all_gather | solution.py:18
  48.1 4.3 %while.109 = (s32[]{:T(128)}, f32[256]{0:T(256)}, s32[]{:T(128)}, f32[4,256]{1,0:T(4,128)S(1)}, f32[4,256]{1,0:T(4,128)S(1)}, /*index=5*/s32[]{:T(128)}, s32[]{:T(128)}, s32[]{:T(128)}, s32[]{:T(128)}) while((s32[]{:T(128)}, f32[256]{0:T(256)}, s32[]{:T(128)}, f32[4,256]{1,0:T(4,128)S(1)}, f32[4,256]{1,0:T(4,128)S(1)}, ...), condition=%wide.region_3.4_spmd.clone, body=%wide.region_2.3_spmd.clone.sunk | while | flops 1032 | bytes 8363 | solution.py:31
  48.7 1.2 add_select_fusion.13
  49.9 1.2 add_select_fusion.13
  51.2 1.2 add_select_fusion.13
  52.4 4.7 %collective-permute-start.2 = (f32[6,16,128]{2,1,0:T(8,128)S(1)}, f32[6,16,128]{2,1,0:T(8,128)S(1)}, u32[]{:S(2)}, u32[]{:S(2)}) collective-permute-start(f32[6,16,128]{2,1,0:T(8,128)S(1)} %get-tuple-element.1214), channel_id=1, source_target_pairs={{1,0},{2,1},{3,2},{4,3},{5,4},{6,5},{7,6},{0,7},{9,8},{10,9},{11,1... | collective-permute-start | bytes 147464 | tf_op jit(solution)/shard_map/ppermute | solution.py:47
  59.1 5.2 %all-gather.1 = f32[1,64,256]{2,1,0:T(8,128)S(1)} all-gather(f32[1,16,256]{2,1,0:T(8,128)S(1)} %get-tuple-element.1172), channel_id=3, replica_groups=mesh['gz'=4,'gx'=8] {'gz'}, dimensions={1}, use_global_device_ids=true | all-gather | bytes 81920 | tf_op jit(solution)/shard_map/all_gather | solution.py:148
  70.0 4.8 %collective-permute-start.4 = (f32[6,16,128]{2,1,0:T(8,128)S(1)}, f32[6,16,128]{2,1,0:T(8,128)S(1)}, u32[]{:S(2)}, u32[]{:S(2)}) collective-permute-start(f32[6,16,128]{2,1,0:T(8,128)S(1)} %get-tuple-element.1193), channel_id=1, source_target_pairs={{1,0},{2,1},{3,2},{4,3},{5,4},{6,5},{7,6},{0,7},{9,8},{10,9},{11,1... | collective-permute-start | bytes 147464 | tf_op jit(solution)/shard_map/ppermute | solution.py:47
  75.4 5.7 %all-gather.2 = f32[1,64,256]{2,1,0:T(8,128)} all-gather(f32[1,16,256]{2,1,0:T(8,128)S(1)} %get-tuple-element.1188), channel_id=4, replica_groups=mesh['gz'=4,'gx'=8] {'gz'}, dimensions={1}, use_global_device_ids=true | all-gather | bytes 81920 | tf_op jit(solution)/shard_map/all_gather | solution.py:148
  81.6 1.5 broadcast_multiply_fusion
  83.3 1.6 fusion.81
  92.5 5.1 %all-gather.7 = f32[4,1,256]{2,1,0:T(1,128)S(1)} all-gather(f32[1,1,256]{2,1,0:T(1,128)S(1)} %add_bitcast_fusion.2), channel_id=1, replica_groups=mesh['gz'=4,'gx'=8] {'gz'}, dimensions={0}, use_global_device_ids=true | all-gather | bytes 5120 | tf_op jit(solution)/shard_map/all_gather | solution.py:18
  97.9 4.4 %collective-permute-start.7 = (f32[6,16,128]{2,1,0:T(8,128)S(1)}, f32[6,16,128]{2,1,0:T(8,128)S(1)}, u32[]{:S(2)}, u32[]{:S(2)}) collective-permute-start(f32[6,16,128]{2,1,0:T(8,128)S(1)} %get-tuple-element.1127), channel_id=1, source_target_pairs={{0,7},{1,0},{2,1},{3,2},{4,3},{5,4},{6,5},{7,6},{8,15},{9,8},{10,9... | collective-permute-start | bytes 147464 | tf_op jit(solution)/shard_map/ppermute | solution.py:36
  102.3 6.7 %collective-permute-done.6 = f32[6,16,128]{2,1,0:T(8,128)S(1)} collective-permute-done((f32[6,16,128]{2,1,0:T(8,128)S(1)}, f32[6,16,128]{2,1,0:T(8,128)S(1)}, u32[]{:S(2)}, u32[]{:S(2)}) %collective-permute-start.6) | collective-permute-done | bytes 49184 | tf_op jit(solution)/shard_map/ppermute | solution.py:36
  109.1 9.3 %reduce-scatter.4.cloned.1.call-done = f32[16,256]{1,0:T(8,128)} async-done(((f32[64,256]{1,0:T(8,128)}), f32[16,256]{1,0:T(8,128)}) %reduce-scatter.4.cloned.1.call-update) | async-done | bytes 16400 | tf_op jit(solution)/shard_map/reduce_scatter | solution.py:157
  122.5 1.6 fusion.77
  124.7 2.2 fusion.2
  131.9 1.8 pad.467
  133.7 1.8 pad.468
  135.5 1.3 add.1082
  137.6 1.2 pad.469
  138.8 1.9 pad.470
  140.6 1.3 add.1084
  144.0 1.9 pad.472
  146.6 5.1 %all-gather.8 = f32[4,1,256]{2,1,0:T(1,128)S(1)} all-gather(f32[1,1,256]{2,1,0:T(1,128)S(1)} %add_bitcast_fusion.1), channel_id=1, replica_groups=mesh['gz'=4,'gx'=8] {'gz'}, dimensions={0}, use_global_device_ids=true | all-gather | bytes 5120 | tf_op jit(solution)/shard_map/all_gather | solution.py:18
  152.3 6.7 %while.112 = (s32[]{:T(128)}, f32[256]{0:T(256)}, s32[]{:T(128)}, f32[4,256]{1,0:T(4,128)}, f32[4,256]{1,0:T(4,128)}, /*index=5*/s32[]{:T(128)}, s32[]{:T(128)}) while((s32[]{:T(128)}, f32[256]{0:T(256)}, s32[]{:T(128)}, f32[4,256]{1,0:T(4,128)}, f32[4,256]{1,0:T(4,128)}, /*index=5*/s32[]{:T(128)}, s32[]{:T(128)}) %tuple.459), condition=%wide.region_15.16_spmd.clone, body=%wide.region_14.15_spmd.clone.sunk | while | flops 1028 | bytes 8301 | solution.py:31
  154.2 1.1 add_select_fusion.16
  156.0 1.1 add_select_fusion.16
  157.8 1.1 add_select_fusion.16
  159.0 2.6 convolution_add_fusion.5
  161.6 2.4 convolution_add_fusion.1
  164.9 4.3 %collective-permute-start.9 = (f32[6,16,128]{2,1,0:T(8,128)}, f32[6,16,128]{2,1,0:T(8,128)S(1)}, u32[]{:S(2)}, u32[]{:S(2)}) collective-permute-start(f32[6,16,128]{2,1,0:T(8,128)} %get-tuple-element.1125), channel_id=1, source_target_pairs={{0,7},{1,0},{2,1},{3,2},{4,3},{5,4},{6,5},{7,6},{8,15},{9,8},{10,9... | collective-permute-start | bytes 147464 | tf_op jit(solution)/shard_map/ppermute | solution.py:36
  170.3 6.0 %collective-permute-done.8 = f32[6,16,128]{2,1,0:T(8,128)S(1)} collective-permute-done((f32[6,16,128]{2,1,0:T(8,128)}, f32[6,16,128]{2,1,0:T(8,128)S(1)}, u32[]{:S(2)}, u32[]{:S(2)}) %collective-permute-start.8) | collective-permute-done | bytes 49184 | tf_op jit(solution)/shard_map/ppermute | solution.py:36
  176.4 8.2 %reduce-scatter.6.cloned.1.call-done = f32[16,256]{1,0:T(8,128)} async-done(((f32[64,256]{1,0:T(8,128)}), f32[16,256]{1,0:T(8,128)}) %reduce-scatter.6.cloned.1.call-update) | async-done | bytes 16400 | tf_op jit(solution)/shard_map/reduce_scatter | solution.py:157
  186.0 1.7 multiply_reduce_fusion.1
  187.7 1.3 fusion.88
  194.1 1.6 fusion.73
  199.6 5.1 %all-gather.9 = f32[4,1,256]{2,1,0:T(1,128)S(1)} all-gather(f32[1,1,256]{2,1,0:T(1,128)S(1)} %add_bitcast_fusion), channel_id=1, replica_groups=mesh['gz'=4,'gx'=8] {'gz'}, dimensions={0}, use_global_device_ids=true | all-gather | bytes 5120 | tf_op jit(solution)/shard_map/all_gather | solution.py:18
  204.9 5.1 %all-gather.6 = f32[4,1,256]{2,1,0:T(1,128)S(1)} all-gather(f32[1,1,256]{2,1,0:T(1,128)S(1)} %add_bitcast_fusion.3), channel_id=1, replica_groups=mesh['gz'=4,'gx'=8] {'gz'}, dimensions={0}, use_global_device_ids=true | all-gather | bytes 5120 | tf_op jit(solution)/shard_map/all_gather | solution.py:18
  216.6 1.5 collective-permute-start.10
  219.3 3.3 collective-permute-start.11
  222.9 37.7 %all-reduce.101 = (f32[128,12]{0,1:T(8,128)}, f32[6,128]{1,0:T(8,128)}) all-reduce(f32[128,12]{0,1:T(8,128)S(1)} %copy-done.103, f32[6,128]{1,0:T(8,128)S(1)} %copy-done.113), channel_id=1, replica_groups=mesh['gz'=4,'gx'=8] {'gz','gx'}, use_global_device_ids=true, to_apply=%region_21.22 | all-reduce | flops 2304 | bytes 18432 | tf_op jit(solution)/shard_map/psum | solution.py:239
  262.8 91.0 %all-reduce.104.cloned.1.call-done = f32[128,128]{1,0:T(8,128)} async-done(((f32[128,128]{1,0:T(8,128)}), f32[128,128]{1,0:T(8,128)}) %all-reduce.104.cloned.1.call-update) | async-done | bytes 65552 | tf_op jit(solution)/shard_map/psum | solution.py:239
  353.8 1.5 copy.127
  (645 shorter events, 69.9 us)
Async XLA Ops:
  7.2 29.9 %copy-start = (bf16[128,128]{1,0:T(8,128)(2,1)S(1)}, bf16[128,128]{1,0:T(8,128)(2,1)}, u32[]{:S(2)}) copy-start(bf16[128,128]{1,0:T(8,128)(2,1)} %param.59) | copy-start | bytes 98308
  7.2 23.9 %slice-start = ((f32[6,16,256]{2,1,0:T(8,128)}), f32[1,16,256]{2,1,0:T(8,128)S(1)}, s32[]{:S(2)}) async-start(f32[6,16,256]{2,1,0:T(8,128)} %param.56), calls=%async_computation.7 | async-start | bytes 32768 | tf_op jit(solution)/shard_map/slice | solution.py:182
  7.2 29.1 %copy-start.7 = (f32[6,16,256]{2,1,0:T(8,128)S(1)}, f32[6,16,256]{2,1,0:T(8,128)}, u32[]{:S(2)}) copy-start(f32[6,16,256]{2,1,0:T(8,128)} %param.56) | copy-start | bytes 294916
  7.2 23.7 %copy-start.116 = (s32[256]{0:T(256)S(1)}, s32[256]{0:T(256)}, u32[]{:S(2)}) copy-start(s32[256]{0:T(256)} %param.63) | copy-start | bytes 3076
  7.2 29.4 %copy-start.52 = (bf16[128,12]{0,1:T(8,128)(2,1)S(1)}, bf16[128,12]{0,1:T(8,128)(2,1)}, u32[]{:S(2)}) copy-start(bf16[128,12]{0,1:T(8,128)(2,1)} %param.58) | copy-start | bytes 9220
  7.2 111.2 %reduce-scatter.4.cloned.1.call-start = ((), (), s32[]{:S(2)}) async-start(), calls=%async_computation.3 | async-start | bytes 81920 | tf_op jit(solution)/shard_map/reduce_scatter | solution.py:157
  8.1 28.2 %collective-permute-start = (f32[6,16,128]{2,1,0:T(8,128)S(1)}, f32[6,16,128]{2,1,0:T(8,128)S(1)}, u32[]{:S(2)}, u32[]{:S(2)}) collective-permute-start(f32[6,16,128]{2,1,0:T(8,128)S(1)} %get-tuple-element.1230), channel_id=1, source_target_pairs={{1,0},{2,1},{3,2},{4,3},{5,4},{6,5},{7,6},{0,7},{9,8},{10,9},{11,1... | collective-permute-start | bytes 147464 | tf_op jit(solution)/shard_map/ppermute | solution.py:47
  14.2 22.1 %collective-permute-start.1 = (f32[6,16,128]{2,1,0:T(8,128)S(1)}, f32[6,16,128]{2,1,0:T(8,128)S(1)}, u32[]{:S(2)}, u32[]{:S(2)}) collective-permute-start(f32[6,16,128]{2,1,0:T(8,128)S(1)} %get-tuple-element.1231), channel_id=1, source_target_pairs={{0,1},{1,2},{2,3},{3,4},{4,5},{5,6},{6,7},{7,0},{8,9},{9,10},{10,1... | collective-permute-start | bytes 147464 | tf_op jit(solution)/shard_map/ppermute | solution.py:46
  14.9 26.7 %copy-start.55 = (f32[256]{0:T(256)}, f32[256]{0:T(256)S(1)}, u32[]{:S(2)}) copy-start(f32[256]{0:T(256)S(1)} %get-tuple-element.1104) | copy-start | bytes 3076
  14.9 77.6 %copy-start.49 = (f32[256]{0:T(256)}, f32[256]{0:T(256)S(1)}, u32[]{:S(2)}) copy-start(f32[256]{0:T(256)S(1)} %get-tuple-element.1105) | copy-start | bytes 3076
  15.7 25.9 %copy-start.80 = (f32[256]{0:T(256)}, f32[256]{0:T(256)S(1)}, u32[]{:S(2)}) copy-start(f32[256]{0:T(256)S(1)} %get-tuple-element.1276) | copy-start | bytes 3076
  15.7 105.5 %copy-start.38 = (f32[256]{0:T(256)}, f32[256]{0:T(256)S(1)}, u32[]{:S(2)}) copy-start(f32[256]{0:T(256)S(1)} %get-tuple-element.1275) | copy-start | bytes 3076
  30.8 88.3 %copy-start.23 = (f32[16,256]{1,0:T(8,128)}, f32[16,256]{1,0:T(8,128)S(1)}, u32[]{:S(2)}) copy-start(f32[16,256]{1,0:T(8,128)S(1)} %get-tuple-element.1103) | copy-start | bytes 49156
  52.4 11.9 %collective-permute-start.2 = (f32[6,16,128]{2,1,0:T(8,128)S(1)}, f32[6,16,128]{2,1,0:T(8,128)S(1)}, u32[]{:S(2)}, u32[]{:S(2)}) collective-permute-start(f32[6,16,128]{2,1,0:T(8,128)S(1)} %get-tuple-element.1214), channel_id=1, source_target_pairs={{1,0},{2,1},{3,2},{4,3},{5,4},{6,5},{7,6},{0,7},{9,8},{10,9},{11,1... | collective-permute-start | bytes 147464 | tf_op jit(solution)/shard_map/ppermute | solution.py:47
  57.1 7.2 %collective-permute-start.3 = (f32[6,16,128]{2,1,0:T(8,128)S(1)}, f32[6,16,128]{2,1,0:T(8,128)S(1)}, u32[]{:S(2)}, u32[]{:S(2)}) collective-permute-start(f32[6,16,128]{2,1,0:T(8,128)S(1)} %get-tuple-element.1215), channel_id=1, source_target_pairs={{0,1},{1,2},{2,3},{3,4},{4,5},{5,6},{6,7},{7,0},{8,9},{9,10},{10,1... | collective-permute-start | bytes 147464 | tf_op jit(solution)/shard_map/ppermute | solution.py:46
  67.3 14.3 %copy-start.9 = (f32[6,16,256]{2,1,0:T(8,128)S(1)}, f32[6,16,256]{2,1,0:T(8,128)}, u32[]{:S(2)}) copy-start(f32[6,16,256]{2,1,0:T(8,128)} %param.57) | copy-start | bytes 294916
  68.7 14.4 %copy-start.92 = (f32[256]{0:T(256)S(1)}, f32[256]{0:T(256)}, u32[]{:S(2)}) copy-start(f32[256]{0:T(256)} %copy-done.90) | copy-start | bytes 3076
  68.7 14.5 %copy-start.56 = (f32[256]{0:T(256)S(1)}, f32[256]{0:T(256)}, u32[]{:S(2)}) copy-start(f32[256]{0:T(256)} %copy-done.55) | copy-start | bytes 3076
  68.7 14.6 %copy-start.81 = (f32[256]{0:T(256)S(1)}, f32[256]{0:T(256)}, u32[]{:S(2)}) copy-start(f32[256]{0:T(256)} %copy-done.80) | copy-start | bytes 3076
  70.0 11.1 %collective-permute-start.4 = (f32[6,16,128]{2,1,0:T(8,128)S(1)}, f32[6,16,128]{2,1,0:T(8,128)S(1)}, u32[]{:S(2)}, u32[]{:S(2)}) collective-permute-start(f32[6,16,128]{2,1,0:T(8,128)S(1)} %get-tuple-element.1193), channel_id=1, source_target_pairs={{1,0},{2,1},{3,2},{4,3},{5,4},{6,5},{7,6},{0,7},{9,8},{10,9},{11,1... | collective-permute-start | bytes 147464 | tf_op jit(solution)/shard_map/ppermute | solution.py:47
  74.8 6.8 %collective-permute-start.5 = (f32[6,16,128]{2,1,0:T(8,128)S(1)}, f32[6,16,128]{2,1,0:T(8,128)S(1)}, u32[]{:S(2)}, u32[]{:S(2)}) collective-permute-start(f32[6,16,128]{2,1,0:T(8,128)S(1)} %get-tuple-element.1194), channel_id=1, source_target_pairs={{0,1},{1,2},{2,3},{3,4},{4,5},{5,6},{6,7},{7,0},{8,9},{9,10},{10,1... | collective-permute-start | bytes 147464 | tf_op jit(solution)/shard_map/ppermute | solution.py:46
  91.6 27.6 %copy-start.62 = (f32[256]{0:T(256)S(1)}, f32[256]{0:T(256)}, u32[]{:S(2)}) copy-start(f32[256]{0:T(256)} %copy-done.60) | copy-start | bytes 3076
  91.9 27.3 %copy-start.93 = (f32[256]{0:T(256)S(1)}, f32[256]{0:T(256)}, u32[]{:S(2)}) copy-start(f32[256]{0:T(256)} %copy-done.90) | copy-start | bytes 3076
  91.9 29.4 %copy-start.82 = (f32[256]{0:T(256)S(1)}, f32[256]{0:T(256)}, u32[]{:S(2)}) copy-start(f32[256]{0:T(256)} %copy-done.80) | copy-start | bytes 3076
  91.9 32.8 %copy-start.66 = (bf16[6,128]{1,0:T(8,128)(2,1)S(1)}, bf16[6,128]{1,0:T(8,128)(2,1)}, u32[]{:S(2)}) copy-start(bf16[6,128]{1,0:T(8,128)(2,1)} %param.60) | copy-start | bytes 4612
  97.8 26.3 %copy-start.32 = (f32[4,256]{1,0:T(4,128)}, f32[4,256]{1,0:T(4,128)S(1)}, u32[]{:S(2)}) copy-start(f32[4,256]{1,0:T(4,128)S(1)} %get-tuple-element.1647) | copy-start | bytes 12292
  97.8 86.7 %reduce-scatter.6.cloned.1.call-start = ((), (), s32[]{:S(2)}) async-start(), calls=%async_computation.4 | async-start | bytes 81920 | tf_op jit(solution)/shard_map/reduce_scatter | solution.py:157
  97.9 11.2 %collective-permute-start.7 = (f32[6,16,128]{2,1,0:T(8,128)S(1)}, f32[6,16,128]{2,1,0:T(8,128)S(1)}, u32[]{:S(2)}, u32[]{:S(2)}) collective-permute-start(f32[6,16,128]{2,1,0:T(8,128)S(1)} %get-tuple-element.1127), channel_id=1, source_target_pairs={{0,7},{1,0},{2,1},{3,2},{4,3},{5,4},{6,5},{7,6},{8,15},{9,8},{10,9... | collective-permute-start | bytes 147464 | tf_op jit(solution)/shard_map/ppermute | solution.py:36
  102.3 6.8 %collective-permute-start.6 = (f32[6,16,128]{2,1,0:T(8,128)S(1)}, f32[6,16,128]{2,1,0:T(8,128)S(1)}, u32[]{:S(2)}, u32[]{:S(2)}) collective-permute-start(f32[6,16,128]{2,1,0:T(8,128)S(1)} %get-tuple-element.1128), channel_id=1, source_target_pairs={{0,1},{1,2},{2,3},{3,4},{4,5},{5,6},{6,7},{7,0},{8,9},{9,10},{10,1... | collective-permute-start | bytes 147464 | tf_op jit(solution)/shard_map/ppermute | solution.py:36
  144.0 15.0 %copy-start.68 = (f32[16,256]{1,0:T(8,128)}, f32[16,256]{1,0:T(8,128)S(1)}, u32[]{:S(2)}) copy-start(f32[16,256]{1,0:T(8,128)S(1)} %pad.471) | copy-start | bytes 49156
  161.6 23.6 %copy-start.24 = (f32[16,256]{1,0:T(8,128)S(1)}, f32[16,256]{1,0:T(8,128)}, u32[]{:S(2)}) copy-start(f32[16,256]{1,0:T(8,128)} %copy-done.23) | copy-start | bytes 49156
  164.9 34.4 %copy-start.57 = (f32[256]{0:T(256)S(1)}, f32[256]{0:T(256)}, u32[]{:S(2)}) copy-start(f32[256]{0:T(256)} %copy-done.55) | copy-start | bytes 3076
  164.9 34.6 %copy-start.51 = (f32[256]{0:T(256)S(1)}, f32[256]{0:T(256)}, u32[]{:S(2)}) copy-start(f32[256]{0:T(256)} %copy-done.49) | copy-start | bytes 3076
  164.9 39.8 %copy-start.33 = (f32[4,256]{1,0:T(4,128)S(1)}, f32[4,256]{1,0:T(4,128)}, u32[]{:S(2)}) copy-start(f32[4,256]{1,0:T(4,128)} %get-tuple-element.1648) | copy-start | bytes 12292
  164.9 39.8 %copy-start.98 = (f32[256]{0:T(256)S(1)}, f32[256]{0:T(256)}, u32[]{:S(2)}) copy-start(f32[256]{0:T(256)} %custom-call.5) | copy-start | bytes 3076
  164.9 45.1 %copy-start.94 = (f32[256]{0:T(256)S(1)}, f32[256]{0:T(256)}, u32[]{:S(2)}) copy-start(f32[256]{0:T(256)} %custom-call.2) | copy-start | bytes 3076
  164.9 95.8 %reduce-scatter.8.cloned.1.call-start = ((), (), s32[]{:S(2)}) async-start(), calls=%async_computation.5 | async-start | bytes 81920 | tf_op jit(solution)/shard_map/reduce_scatter | solution.py:157
  164.9 11.4 %collective-permute-start.9 = (f32[6,16,128]{2,1,0:T(8,128)}, f32[6,16,128]{2,1,0:T(8,128)S(1)}, u32[]{:S(2)}, u32[]{:S(2)}) collective-permute-start(f32[6,16,128]{2,1,0:T(8,128)} %get-tuple-element.1125), channel_id=1, source_target_pairs={{0,7},{1,0},{2,1},{3,2},{4,3},{5,4},{6,5},{7,6},{8,15},{9,8},{10,9... | collective-permute-start | bytes 147464 | tf_op jit(solution)/shard_map/ppermute | solution.py:36
  169.3 7.0 %collective-permute-start.8 = (f32[6,16,128]{2,1,0:T(8,128)}, f32[6,16,128]{2,1,0:T(8,128)S(1)}, u32[]{:S(2)}, u32[]{:S(2)}) collective-permute-start(f32[6,16,128]{2,1,0:T(8,128)} %get-tuple-element.1126), channel_id=1, source_target_pairs={{0,1},{1,2},{2,3},{3,4},{4,5},{5,6},{6,7},{7,0},{8,9},{9,10},{10,1... | collective-permute-start | bytes 147464 | tf_op jit(solution)/shard_map/ppermute | solution.py:36
  170.3 40.1 %copy-start.67 = (bf16[6,128]{1,0:T(8,128)(2,1)S(1)}, bf16[6,128]{1,0:T(8,128)(2,1)}, u32[]{:S(2)}) copy-start(bf16[6,128]{1,0:T(8,128)(2,1)} %param.60) | copy-start | bytes 4612
  210.2 143.6 %all-reduce.104.cloned.1.call-start = ((), (), s32[]{:S(2)}) async-start(), calls=%async_computation.6 | async-start | bytes 131072 | tf_op jit(solution)/shard_map/psum | solution.py:239
  215.5 45.9 %copy-start.63 = (f32[256]{0:T(256)S(1)}, f32[256]{0:T(256)}, u32[]{:S(2)}) copy-start(f32[256]{0:T(256)} %copy-done.60) | copy-start | bytes 3076
  215.5 45.9 %copy-start.74 = (f32[16,256]{1,0:T(8,128)S(1)}, f32[16,256]{1,0:T(8,128)}, u32[]{:S(2)}) copy-start(f32[16,256]{1,0:T(8,128)} %copy-done.73) | copy-start | bytes 49156
  215.5 45.9 %copy-start.76 = (f32[16,256]{1,0:T(8,128)S(1)}, f32[16,256]{1,0:T(8,128)}, u32[]{:S(2)}) copy-start(f32[16,256]{1,0:T(8,128)} %copy-done.75) | copy-start | bytes 49156
  215.6 45.9 %copy-start.100 = (f32[256]{0:T(256)S(1)}, f32[256]{0:T(256)}, u32[]{:S(2)}) copy-start(f32[256]{0:T(256)} %copy-done.99) | copy-start | bytes 3076
  215.6 45.9 %copy-start.10 = (f32[6,16,256]{2,1,0:T(8,128)S(1)}, f32[6,16,256]{2,1,0:T(8,128)}, u32[]{:S(2)}) copy-start(f32[6,16,256]{2,1,0:T(8,128)} %param.57) | copy-start | bytes 294916
  216.6 44.0 %collective-permute-start.10 = (f32[6,16,128]{2,1,0:T(8,128)S(1)}, f32[6,16,128]{2,1,0:T(8,128)S(1)}, u32[]{:S(2)}, u32[]{:S(2)}) collective-permute-start(f32[6,16,128]{2,1,0:T(8,128)S(1)} %get-tuple-element.1124), channel_id=1, source_target_pairs={{0,1},{1,2},{2,3},{3,4},{4,5},{5,6},{6,7},{7,0},{8,9},{9,10},{10,1... | collective-permute-start | bytes 147464 | tf_op jit(solution)/shard_map/ppermute | solution.py:36
  219.3 41.3 %collective-permute-start.11 = (f32[6,16,128]{2,1,0:T(8,128)S(1)}, f32[6,16,128]{2,1,0:T(8,128)S(1)}, u32[]{:S(2)}, u32[]{:S(2)}) collective-permute-start(f32[6,16,128]{2,1,0:T(8,128)S(1)} %get-tuple-element.1123), channel_id=1, source_target_pairs={{0,7},{1,0},{2,1},{3,2},{4,3},{5,4},{6,5},{7,6},{8,15},{9,8},{10,9... | collective-permute-start | bytes 147464 | tf_op jit(solution)/shard_map/ppermute | solution.py:36
  (90 other events, 311.3 us)
Sparse Core Ops, SparseCore 0:
  98.0 20.4 reduce-scatter.3
  165.0 19.4 reduce-scatter.5
  210.4 19.4 reduce-scatter.7
  236.3 117.5 all-reduce.103
where the time goes:
time: 365 us; the launch traced here: 362 us
  waiting for transfers between devices  122 us (33%)
  blocking collectives  89.4 us (24%)
  other arithmetic  41.4 us (11%)
  local copies, waits for them, and re-layouts  34.2 us (9%)
  starting transfers between devices  29.2 us (8%)
  matrix products  29 us (8%)
  between operations  16.4 us (4%)
    psum x1, waiting for transfers between devices, on_device(): lax.psum((TIME_STEP * (grads_two[0] + grads_one[0] + grads_zero[0]), TIME...  91 us
    psum x1, blocking collectives, on_device(): lax.psum((TIME_STEP * (grads_two[0] + grads_one[0] + grads_zero[0]), TIME...  37.7 us
    all_gather x7, blocking collectives, prefix(): everything = jax.tree.map(lambda part: lax.all_gather(part, axis), shard)  35.5 us
    reduce_scatter x3, waiting for transfers between devices, heating_adjoint(): lax.psum_scatter(lax.dot_general(own_rows, lead_theta, (((0,), (0,)), (()...  17.5 us
    dot_general x18, matrix products, contract(): lax.dot_general(left, right, (((left_dim,), (right_dim,)), ((), ())), pre...  17.1 us
    all_gather x3, blocking collectives, heating(): lax.all_gather(theta, 'gz', axis=0, tiled=True)  16.2 us
    ppermute x3, starting transfers between devices, padded_2(): after = lax.ppermute(first, axis, down)  15.5 us
    ppermute x6, starting transfers between devices, passed_along(): lax.ppermute(shard, axis, [(i, (i + by) % length) for i in range(length)])  13.5 us
  transfers between devices with their start and end apart: 16, of which 6 were waited for; matrix products, arithmetic and copies ran while one was open for 5% of the time, Pallas kernels for 0%

commit v1 on v0

v1 whole, which is shorter than its diff:
```python
import functools

import jax
import jax.numpy as jnp
from jax import lax
from jax.experimental import pallas as pl
from jax.experimental.pallas import tpu as pltpu
from jax.sharding import PartitionSpec as P

NF = 6
NY = 64
LANES = 128
MESH = pl.DeviceIdType.MESH
F32 = jnp.float32
BF16 = jnp.bfloat16


def mm(a, b, precision=None):
    return lax.dot_general(
        a, b, (((1,), (0,)), ((), ())), precision=precision, preferred_element_type=F32
    )


def mm_t(a, b, precision=None):
    return lax.dot_general(
        a, b, (((1,), (1,)), ((), ())), precision=precision, preferred_element_type=F32
    )


def iota(shape, dim):
    return lax.broadcasted_iota(jnp.int32, shape, dim)


def kernel(
    nz, nx, levels, hid, share,
    state, cot, w_in, w_mid, w_out, rad, fall, act,
    new_state, state_grad, g_mid, g_in, g_out,
    sp, lp, gp, tg, tl, dxs, dys, moved, feats, out_cot, t1s, t2s, h1s, h2s,
    k1, k1t, k2, k2t, wmt, pre1, pre2, by_in, by_out, radt, tab, fcs, acc, a_in, a_out, a_mid,
    pack, part, parts, full,
    halo_send, halo_recv, gz_send, gz_recv, rs_send, rs_recv, ag_send, ag_recv, fin_send, fin_recv,
):
    mz, mx = lax.axis_index("gz"), lax.axis_index("gx")
    left, right = lax.rem(mx + nx - 1, nx), lax.rem(mx + 1, nx)
    rows_all = levels * hid

    barrier = pltpu.get_barrier_semaphore()
    for o in range(1, nz):
        pl.semaphore_signal(
            barrier, inc=1, device_id=(lax.rem(mz + o, nz), mx), device_id_type=MESH
        )
    for o in range(1, nx):
        pl.semaphore_signal(
            barrier, inc=1, device_id=(mz, lax.rem(mx + o, nx)), device_id_type=MESH
        )

    def spread(rows, cols):
        return (iota((rows, cols), 1) // levels == iota((rows, cols), 0)).astype(F32).astype(BF16)

    def spread_t(rows, cols):
        return (iota((rows, cols), 0) // levels == iota((rows, cols), 1)).astype(F32).astype(BF16)

    eye = (iota((hid, hid), 0) == iota((hid, hid), 1)).astype(F32).astype(BF16)
    w1 = mm(w_in[...], spread(2 * NF, 2 * NF * levels))
    w1t = mm_t(spread_t(2 * NF * levels, 2 * NF), w_in[...])
    w2 = mm(spread_t(NF * levels, NF), w_out[...])
    w2t = mm_t(eye, w2.astype(BF16))
    wmt[...] = mm_t(eye, w_mid[...]).astype(BF16)

    def place(z, carry):
        rows = pl.ds(pl.multiple_of(z * hid, hid), hid)
        k1[rows, :] = jnp.where(iota(w1.shape, 1) % levels == z, w1, 0.0).astype(BF16)
        k2t[rows, :] = jnp.where(iota(w2t.shape, 1) % levels == z, w2t, 0.0).astype(BF16)
        k1t[:, rows] = jnp.where(iota(w1t.shape, 0) % levels == z, w1t, 0.0).astype(BF16)
        k2[:, rows] = jnp.where(iota(w2.shape, 0) % levels == z, w2, 0.0).astype(BF16)
        return carry

    lax.fori_loop(0, levels, place, 0)
    radt[...] = rad[...].T

    columns = 2 * LANES
    shape = (levels, columns)
    rate = jnp.broadcast_to(fall[...], shape)
    r1 = rate / (1.0 + rate)
    r2 = r1 * r1
    r4 = r2 * r2
    r8 = r4 * r4
    powers = [r1, r2, r4, r8, r8 * r8]
    up, down = jnp.ones(shape, F32), jnp.ones(shape, F32)
    level = iota(shape, 0)
    for bit in range(5):
        up = jnp.where(((level + 1) // (1 << bit)) % 2 == 1, up * powers[bit], up)
        down = jnp.where(((levels - level) // (1 << bit)) % 2 == 1, down * powers[bit], down)
    for at, value in enumerate(
        powers + [1.0 / (1.0 + rate), jnp.broadcast_to(act[...].astype(F32), shape), down, up]
    ):
        tab[at] = value

    for c in range(2):
        lanes = slice(c * LANES, (c + 1) * LANES)
        sp[0, c + 1] = state[:, :, lanes]
        lp[0, c + 1] = (2.0 / 3.0) * cot[:, :, lanes]
        acc[c] = cot[:, :, lanes] / 3.0
    a_in[...] = jnp.zeros_like(a_in)
    a_out[...] = jnp.zeros_like(a_out)
    a_mid[...] = jnp.zeros_like(a_mid)

    pl.semaphore_wait(barrier, nz - 1 + nx - 1)

    def halo(buf, kind, k):
        return [
            pltpu.make_async_remote_copy(
                src_ref=buf.at[k, 1], dst_ref=buf.at[k, 3],
                send_sem=halo_send.at[kind, k, 0], recv_sem=halo_recv.at[kind, k, 0],
                device_id=(mz, left), device_id_type=MESH,
            ),
            pltpu.make_async_remote_copy(
                src_ref=buf.at[k, 2], dst_ref=buf.at[k, 0],
                send_sem=halo_send.at[kind, k, 1], recv_sem=halo_recv.at[kind, k, 1],
                device_id=(mz, right), device_id_type=MESH,
            ),
        ]

    def level_copies(buf, kind, k):
        sends, receives = [], []
        for o in range(1, nz):
            peer, source = lax.rem(mz + o, nz), lax.rem(mz + nz - o, nz)
            sends.append(
                pltpu.make_async_remote_copy(
                    src_ref=buf.at[k, mz], dst_ref=buf.at[k, mz],
                    send_sem=gz_send.at[kind, k, o], recv_sem=gz_recv.at[kind, k, mz],
                    device_id=(peer, mx), device_id_type=MESH,
                )
            )
            receives.append(
                pltpu.make_async_remote_copy(
                    src_ref=buf.at[k, mz], dst_ref=buf.at[k, source],
                    send_sem=gz_send.at[kind, k, o], recv_sem=gz_recv.at[kind, k, source],
                    device_id=(peer, mx), device_id_type=MESH,
                )
            )
        return sends, receives

    lane = iota((1, levels, LANES), 2)
    low = lane < NY
    y_last, y_first = lane % NY == NY - 1, lane % NY == 0
    depth = iota((levels, LANES), 0)

    def along_x(chunks):
        turned = [pltpu.roll(chunk, NY, 2) for chunk in chunks]
        out = []
        for i in (1, 2):
            plus = jnp.where(low, turned[i], turned[i + 1])
            minus = jnp.where(low, turned[i - 1], turned[i])
            out.append((plus, minus, (8.0 * (plus - minus) - (chunks[i + 1] - chunks[i - 1])) / 12.0))
        return out

    def along_y(chunk):
        plus = jnp.where(y_last, pltpu.roll(chunk, NY - 1, 2), pltpu.roll(chunk, LANES - 1, 2))
        minus = jnp.where(y_first, pltpu.roll(chunk, NY + 1, 2), pltpu.roll(chunk, 1, 2))
        return plus, minus

    def settle(source, lanes, downward):
        value = tab[5, :, lanes] * source
        for bit in range(4):
            step = 1 << bit
            if downward:
                moved_by = pltpu.roll(value, levels - step, 0)
                inside = depth < levels - step
            else:
                moved_by = pltpu.roll(value, step, 0)
                inside = depth >= step
            value = value + tab[bit, :, lanes] * jnp.where(inside, moved_by, 0.0)
        return value

    def inflow(buf, k, lanes, downward):
        total = jnp.zeros((8, LANES), F32)
        order = range(nz - 1, 0, -1) if downward else range(nz - 1)
        for j in order:
            reached = j > mz if downward else j < mz
            following = buf[k, j, levels:, lanes] + tab[4, 0:8, lanes] * total
            total = jnp.where(reached, following, total)
        return total[0:1]

    def chunk_lanes(c):
        return slice(c * LANES, (c + 1) * LANES)

    def forward(k, carry):
        own = [sp[k, 1], sp[k, 2]]
        halos = halo(sp, 0, k)
        for copy in halos:
            copy.start()
        local = []
        for c in range(2):
            value = settle(own[c][5], chunk_lanes(c), True)
            local.append(value)
            tg[k, mz, 0:levels, chunk_lanes(c)] = own[c][3]
            tg[k, mz, levels:, chunk_lanes(c)] = jnp.broadcast_to(value[0:1], (8, LANES))
        sends, receives = level_copies(tg, 0, k)
        for copy in sends:
            copy.start()
        for copy in halos:
            copy.wait_recv()
        x_sides = along_x([sp[k, 0], own[0], own[1], sp[k, 3]])
        for c in range(2):
            y_plus, y_minus = along_y(own[c])
            x_plus, x_minus, deriv_x = x_sides[c]
            deriv_y = (y_plus - y_minus) / 2.0
            laplace = x_plus + x_minus + y_plus + y_minus - 4.0 * own[c]
            dxs[k, c] = deriv_x
            dys[k, c] = deriv_y
            moved[c] = -(own[c][0:1] * deriv_x + own[c][1:2] * deriv_y) + 0.1 * laplace
            feats[k, 0 : NF * levels, chunk_lanes(c)] = (
                own[c].reshape(NF * levels, LANES).astype(BF16)
            )
            feats[k, NF * levels :, chunk_lanes(c)] = (
                deriv_x.reshape(NF * levels, LANES).astype(BF16)
            )

        def layers(group, inner):
            for j in range(4):
                rows = pl.ds(pl.multiple_of((group * 4 + j) * hid, hid), hid)
                t1 = jnp.tanh(mm(k1[rows, :], feats[k]))
                t1s[k, rows, :] = t1
                h1 = t1.astype(BF16)
                h1s[k, rows, :] = h1
                t2 = jnp.tanh(mm(w_mid[...], h1))
                t2s[k, rows, :] = t2
                h2s[k, rows, :] = t2.astype(BF16)
            return inner

        lax.fori_loop(0, levels // 4, layers, 0)
        closure = mm(k2[...], h2s[k])
        for copy in receives:
            copy.wait_recv()
        heat = mm(
            rad[pl.ds(pl.multiple_of(mz * levels, levels), levels), :],
            tg[k, :, 0:levels, :].reshape(nz * levels, columns),
            lax.Precision.HIGHEST,
        )
        keep = jnp.where(k == 0, 0.0, jnp.where(k == 1, 0.75, 1.0 / 3.0))
        take = jnp.where(k == 0, 1.0, jnp.where(k == 1, 0.25, 2.0 / 3.0))
        for c in range(2):
            lanes = chunk_lanes(c)
            total = moved[c] + closure[:, lanes].reshape(NF, levels, LANES)
            fallen = local[c] + tab[7, :, lanes] * inflow(tg, k, lanes, True)
            total = jnp.concatenate(
                [
                    total[0:3],
                    total[3:4] + heat[:, lanes][None],
                    total[4:5],
                    total[5:6] + (tab[6, :, lanes] * (fallen - own[c][5]))[None],
                ],
                0,
            )
            sp[k + 1, c + 1] = keep * state[:, :, lanes] + take * (own[c] + 0.25 * total)
        for copy in halos + sends:
            copy.wait_send()
        return carry

    lax.fori_loop(0, 3, forward, 0)
    for c in range(2):
        new_state[:, :, chunk_lanes(c)] = sp[3, c + 1]


    def gathered(cols):
        at = iota((levels * 16, cols), 0)
        return ((at % 16) * levels + at // 16 == iota((levels * 16, cols), 1)).astype(F32).astype(BF16)

    def backward(i, carry):
        k = 2 - i
        lam = [lp[i, 1], lp[i, 2]]
        halos = halo(lp, 1, i)
        for copy in halos:
            copy.start()
        local, masked = [], []
        for c in range(2):
            lanes = chunk_lanes(c)
            source = tab[6, :, lanes] * lam[c][5]
            value = settle(source, lanes, False)
            masked.append(source)
            local.append(value)
            tl[i, mz, 0:levels, lanes] = lam[c][3]
            tl[i, mz, levels:, lanes] = jnp.broadcast_to(value[levels - 1 : levels], (8, LANES))
            out_cot[:, lanes] = lam[c].reshape(NF * levels, LANES).astype(BF16)
        sends, receives = level_copies(tl, 1, i)
        for copy in sends:
            copy.start()

        def layers(group, inner):
            for j in range(4):
                rows = pl.ds(pl.multiple_of((group * 4 + j) * hid, hid), hid)
                t2 = t2s[k, rows, :]
                p2 = (mm(k2t[rows, :], out_cot[...]) * (1.0 - t2 * t2)).astype(BF16)
                pre2[rows, :] = p2
                t1 = t1s[k, rows, :]
                pre1[rows, :] = (mm(wmt[...], p2) * (1.0 - t1 * t1)).astype(BF16)
            return inner

        lax.fori_loop(0, levels // 4, layers, 0)
        feature_cot = mm(k1t[...], pre1[...])
        for c in range(2):
            lanes = chunk_lanes(c)
            fcs[c] = feature_cot[0 : NF * levels, lanes].reshape(NF, levels, LANES)
            gp[i, c + 1] = (
                feature_cot[NF * levels :, lanes].reshape(NF, levels, LANES)
                - sp[k, c + 1, 0:1] * lp[i, c + 1]
            )
        rims = halo(gp, 2, i)
        for copy in rims:
            copy.start()

        by_in[...] = mm(gathered(2 * NF * levels), feats[k]).astype(BF16)
        by_out[...] = mm(gathered(NF * levels), out_cot[...]).astype(BF16)

        def terms(group, inner):
            s_in, s_out, s_mid = inner
            for j in range(4):
                z = group * 4 + j
                rows = pl.ds(pl.multiple_of(z * hid, hid), hid)
                few = pl.ds(pl.multiple_of(z * 16, 16), 16)
                s_mid = s_mid + mm_t(pre2[rows, :], h1s[k, rows, :])
                s_in = s_in + mm_t(by_in[few, :], pre1[rows, :])
                s_out = s_out + mm_t(by_out[few, :], h2s[k, rows, :])
            return s_in, s_out, s_mid

        s_in, s_out, s_mid = lax.fori_loop(
            0, levels // 4, terms, (a_in[...], a_out[...], a_mid[...])
        )
        a_in[...] = s_in
        a_out[...] = s_out
        a_mid[...] = s_mid

        for copy in halos:
            copy.wait_recv()
        for copy in receives:
            copy.wait_recv()
        heat = mm(
            radt[pl.ds(pl.multiple_of(mz * levels, levels), levels), :],
            tl[i, :, 0:levels, :].reshape(nz * levels, columns),
            lax.Precision.HIGHEST,
        )
        lam_sides = along_x([lp[i, 0], lam[0], lam[1], lp[i, 3]])
        for copy in rims:
            copy.wait_recv()
        g_sides = along_x([gp[i, 0], gp[i, 1], gp[i, 2], gp[i, 3]])
        weight = jnp.where(k == 0, 1.0, jnp.where(k == 1, 0.0, 0.75))
        share_on = jnp.where(k == 2, 0.25, 1.0)
        for c in range(2):
            lanes = chunk_lanes(c)
            now = lam[c]
            y_plus, y_minus = along_y(now)
            x_plus, x_minus, _ = lam_sides[c]
            carried_plus, carried_minus = along_y(sp[k, c + 1, 1:2] * now)
            back = (
                (carried_plus - carried_minus) / 2.0
                - g_sides[c][2]
                + 0.1 * (x_plus + x_minus + y_plus + y_minus - 4.0 * now)
                + fcs[c]
            )
            pulled = local[c] + tab[8, :, lanes] * inflow(tl, i, lanes, False)
            back = jnp.concatenate(
                [
                    back[0:1] - jnp.sum(now * dxs[k, c], axis=0, keepdims=True),
                    back[1:2] - jnp.sum(now * dys[k, c], axis=0, keepdims=True),
                    back[2:3],
                    back[3:4] + heat[:, lanes][None],
                    back[4:5],
                    back[5:6] + (pulled - masked[c])[None],
                ],
                0,
            )
            whole = now + 0.25 * back
            acc[c] = acc[c] + weight * whole
            lp[i + 1, c + 1] = share_on * whole
        for copy in halos + sends + rims:
            copy.wait_send()
        return carry

    lax.fori_loop(0, 3, backward, 0)
    for c in range(2):
        state_grad[:, :, chunk_lanes(c)] = acc[c]

    total_rows = nz * share
    everything = jnp.concatenate(
        [
            a_mid[...],
            a_in[...],
            a_out[0:8, :],
            jnp.zeros((total_rows - hid - 24, LANES), F32),
        ],
        0,
    )
    pack[...] = everything.reshape(nz, share, LANES)
    scatter = []
    for o in range(1, nz):
        peer = lax.rem(mz + o, nz)
        scatter.append(
            pltpu.make_async_remote_copy(
                src_ref=pack.at[peer], dst_ref=part.at[o],
                send_sem=rs_send.at[o], recv_sem=rs_recv.at[o],
                device_id=(peer, mx), device_id_type=MESH,
            )
        )
    for copy in scatter:
        copy.start()
    mine = pack[mz]
    for o in range(1, nz):
        scatter[o - 1].wait_recv()
        mine = mine + part[o]
    parts[mx] = mine

    sends, receives = [], []
    for o in range(1, nx):
        peer, source = lax.rem(mx + o, nx), lax.rem(mx + nx - o, nx)
        for dst, to in ((mx, sends), (source, receives)):
            to.append(
                pltpu.make_async_remote_copy(
                    src_ref=parts.at[mx], dst_ref=parts.at[dst],
                    send_sem=ag_send.at[o], recv_sem=ag_recv.at[dst],
                    device_id=(mz, peer), device_id_type=MESH,
                )
            )
    for copy in sends:
        copy.start()
    for copy in receives:
        copy.wait_recv()
    summed = parts[0]
    for j in range(1, nx):
        summed = summed + parts[j]
    full[mz] = 0.25 * summed

    sends_z, receives_z = [], []
    for o in range(1, nz):
        peer, source = lax.rem(mz + o, nz), lax.rem(mz + nz - o, nz)
        for dst, to in ((mz, sends_z), (source, receives_z)):
            to.append(
                pltpu.make_async_remote_copy(
                    src_ref=full.at[mz], dst_ref=full.at[dst],
                    send_sem=fin_send.at[o], recv_sem=fin_recv.at[dst],
                    device_id=(peer, mx), device_id_type=MESH,
                )
            )
    for copy in sends_z:
        copy.start()
    for copy in receives_z:
        copy.wait_recv()
    result = full[...].reshape(total_rows, LANES)
    g_mid[...] = result[0:hid]
    g_in[...] = result[hid : hid + 16]
    g_out[...] = result[hid + 16 : hid + 24]
    for copy in scatter + sends + sends_z:
        copy.wait_send()


def on_device(nz, nx, state, state_cot, w_in, w_mid, w_out, radiation, fall_rate, active):
    fields, levels, columns = state.shape
    hid = w_in.shape[0]
    assert fields == NF and columns == 2 * LANES and hid == LANES and levels == 16
    share = -(-(hid + 24) // (8 * nz)) * 8
    cells = levels * hid
    wide = NF * levels
    chunk = (4, NF, levels, LANES)
    two = (2, NF, levels, LANES)
    dma = pltpu.SemaphoreType.DMA
    vmem = pltpu.VMEM
    scratch = [
        vmem((4,) + chunk, F32),
        vmem((4,) + chunk, F32),
        vmem((3,) + chunk, F32),
        vmem((3, nz, levels + 8, columns), F32),
        vmem((3, nz, levels + 8, columns), F32),
        vmem((3,) + two, F32),
        vmem((3,) + two, F32),
        vmem(two, F32),
        vmem((3, 2 * wide, columns), BF16),
        vmem((wide, columns), BF16),
        vmem((3, cells, columns), F32),
        vmem((3, cells, columns), F32),
        vmem((3, cells, columns), BF16),
        vmem((3, cells, columns), BF16),
        vmem((cells, 2 * wide), BF16),
        vmem((2 * wide, cells), BF16),
        vmem((wide, cells), BF16),
        vmem((cells, wide), BF16),
        vmem((hid, hid), BF16),
        vmem((cells, columns), BF16),
        vmem((cells, columns), BF16),
        vmem((levels * 16, columns), BF16),
        vmem((levels * 16, columns), BF16),
        vmem(radiation.shape, F32),
        vmem((9, levels, columns), F32),
        vmem(two, F32),
        vmem(two, F32),
        vmem((16, hid), F32),
        vmem((16, hid), F32),
        vmem((hid, hid), F32),
        vmem((nz, share, LANES), F32),
        vmem((nz, share, LANES), F32),
        vmem((nx, share, LANES), F32),
        vmem((nz, share, LANES), F32),
        dma((3, 3, 2)), dma((3, 3, 2)),
        dma((2, 3, nz)), dma((2, 3, nz)),
        dma((nz,)), dma((nz,)),
        dma((nx,)), dma((nx,)),
        dma((nz,)), dma((nz,)),
    ]
    whole = pl.BlockSpec(memory_space=pltpu.VMEM)
    new_state, state_grad, g_mid, g_in, g_out = pl.pallas_call(
        functools.partial(kernel, nz, nx, levels, hid, share),
        out_shape=(
            jax.ShapeDtypeStruct(state.shape, F32),
            jax.ShapeDtypeStruct(state.shape, F32),
            jax.ShapeDtypeStruct((hid, hid), F32),
            jax.ShapeDtypeStruct((16, hid), F32),
            jax.ShapeDtypeStruct((8, hid), F32),
        ),
        in_specs=[whole] * 8,
        out_specs=[whole] * 5,
        scratch_shapes=scratch,
        compiler_params=pltpu.CompilerParams(
            collective_id=0, has_side_effects=True, vmem_limit_bytes=48 * 1024 * 1024
        ),
        name="adjoint_step",
    )(
        state, state_cot, w_in, w_mid, w_out, radiation,
        fall_rate.reshape(1, columns), active.reshape(1, columns),
    )
    return new_state, state_grad, g_in[: 2 * NF].T, g_mid, g_out[:NF]


def solution(mesh):
    placed = (P(None, "gz", "gx"), P(None, "gz", "gx"), P(), P(), P(), P(), P("gx"), P("gx"))
    return jax.shard_map(
        functools.partial(on_device, mesh.shape["gz"], mesh.shape["gx"]),
        mesh=mesh,
        in_specs=placed,
        out_specs=(P(None, "gz", "gx"), P(None, "gz", "gx"), P(), P(), P()),
        check_vma=False,
    )
```

time: 365 us -> 67.2 us (0.18)
  waiting for transfers between devices: 122 us -> 0 us
  blocking collectives: 89.4 us -> 0 us
  Pallas kernels: 0 us -> 59.6 us
  other arithmetic: 41.4 us -> 0 us
  starting transfers between devices: 29.2 us -> 0 us
  matrix products: 29 us -> 0 us
  local copies, waits for them, and re-layouts: 34.2 us -> 6.49 us
  between operations: 16.4 us -> 0.71 us
    psum x1 -> x0, waiting for transfers between devices: 91 us -> none  [on_device(): lax.psum((TIME_STEP * (grads_two[0] + grads_one[0] + grads_zero[0]), TIME...]
    pallas_call x0 -> x1, Pallas kernels: none -> 59.6 us  [on_device(): pl.pallas_call(functools.partial(kernel, nz, nx, levels, hid, share), out...]
    all_gather x10 -> x0, blocking collectives: 51.7 us -> none  [the longest x7 35.5 us: prefix(): everything = jax.tree.map(lambda part: lax.all_gather(part, axis), shard)]
    psum x1 -> x0, blocking collectives: 37.7 us -> none  [on_device(): lax.psum((TIME_STEP * (grads_two[0] + grads_one[0] + grads_zero[0]), TIME...]
    ppermute x12 -> x0, starting transfers between devices: 29.1 us -> none  [the longest x3 15.5 us: padded_2(): after = lax.ppermute(first, axis, down)]
    dot_general x33 -> x0, matrix products: 29 us -> none  [the longest x18 17.1 us: contract(): lax.dot_general(left, right, (((left_dim,), (right_dim,)), ((), ())), pre...]
    reduce_scatter x3 -> x0, waiting for transfers between devices: 17.5 us -> none  [heating_adjoint(): lax.psum_scatter(lax.dot_general(own_rows, lead_theta, (((0,), (0,)), (()...]
    add x55 -> x0, other arithmetic: 13.3 us -> none  [the longest x23 4.94 us: compose(): return (later[0] * earlier[0], later[1] + later[0] * earlier[1])]
  transfers between devices with their start and end apart: 16 -> 0, of which waited for: 6 -> 0; matrix products, arithmetic and copies ran while one was open for 5% -> 0% of each run, Pallas kernels for 0% -> 0%
where the time goes in v1:
time: 67.2 us; the launch traced here: 66.8 us
  Pallas kernels  59.6 us (89%)
  local copies, waits for them, and re-layouts  6.49 us (10%)
  between operations  0.71 us (1%)
    pallas_call x1, Pallas kernels, on_device(): pl.pallas_call(functools.partial(kernel, nz, nx, levels, hid, share), out...  59.6 us
    unnamed x19, local copies, waits for them, and re-layouts  5.89 us

profile of v1, /device:TPU:0, one launch (start us, length us, event | category | flops | bytes accessed | tf_op | source)
XLA Modules:
  0.0 66.8 jit_solution(17994801692285388351)
XLA Ops:
  0.6 0.0 copy-start.2
  0.6 0.0 copy-start.4
  0.7 0.0 copy-start.5
  0.7 0.0 copy-start.6
  0.7 0.8 %copy.13.w_in = bf16[128,12]{1,0:T(8,128)(2,1)S(1)} copy(bf16[128,12]{0,1:T(8,128)(2,1)} %param.10) | data formatting | bytes 6144 | tf_op args[2]
  1.5 0.0 copy-done.2
  1.5 0.0 copy-done.4
  1.5 0.0 copy-done.5
  1.5 0.0 copy-done.6
  1.5 0.0 copy-start
  1.6 0.9 %copy-done = f32[6,16,256]{2,1,0:T(8,128)S(1)} copy-done((f32[6,16,256]{2,1,0:T(8,128)S(1)}, f32[6,16,256]{2,1,0:T(8,128)}, u32[]{:S(2)}) %copy-start) | copy-done | bytes 98328
  2.4 0.0 copy-start.1
  2.4 0.9 %copy-done.1 = f32[6,16,256]{2,1,0:T(8,128)S(1)} copy-done((f32[6,16,256]{2,1,0:T(8,128)S(1)}, f32[6,16,256]{2,1,0:T(8,128)}, u32[]{:S(2)}) %copy-start.1) | copy-done | bytes 98328
  3.3 0.0 copy-start.3
  3.3 0.8 %copy-done.3 = f32[64,64]{1,0:T(8,128)S(1)} copy-done((f32[64,64]{1,0:T(8,128)S(1)}, f32[64,64]{1,0:T(8,128)}, u32[]{:S(2)}) %copy-start.3) | copy-done | bytes 16408
  4.1 59.6 %adjoint_step.1 = (f32[6,16,256]{2,1,0:T(8,128)S(1)}, f32[6,16,256]{2,1,0:T(8,128)S(1)}, f32[128,128]{1,0:T(8,128)S(1)}, f32[16,128]{1,0:T(8,128)S(1)}, f32[8,128]{1,0:T(8,128)S(1)}) custom-call(f32[6,16,256]{2,1,0:T(8,128)S(1)} %copy-done, f32[6,16,256]{2,1,0:T(8,128)S(1)} %copy-done.1, bf16[128,12]{1,0:T(8,128)(2,1)S(1)} %copy.13.w_in, ...), custom_call_target="tpu_custom_call" | custom-call | tf_op jit(solution)/shard_map/adjoint_step/pallas_call | solution.py:509
  63.7 0.6 slice_bitcast_fusion
  64.3 0.6 copy.18
  64.9 0.6 copy.19
  65.5 0.6 copy.20
  66.2 0.6 copy.21
Async XLA Ops:
  0.6 0.9 %copy-start.2 = (bf16[128,128]{1,0:T(8,128)(2,1)S(1)}, bf16[128,128]{1,0:T(8,128)(2,1)}, u32[]{:S(2)}) copy-start(bf16[128,128]{1,0:T(8,128)(2,1)} %w_mid.1) | copy-start | bytes 98308
  0.6 0.9 %copy-start.4 = (bf16[6,128]{1,0:T(8,128)(2,1)S(1)}, bf16[6,128]{1,0:T(8,128)(2,1)}, u32[]{:S(2)}) copy-start(bf16[6,128]{1,0:T(8,128)(2,1)} %w_out.1) | copy-start | bytes 4612
  0.7 0.9 %copy-start.5 = (f32[256]{0:T(256)S(1)}, f32[256]{0:T(256)}, u32[]{:S(2)}) copy-start(f32[256]{0:T(256)} %param.14) | copy-start | bytes 3076
  0.7 0.9 %copy-start.6 = (s32[256]{0:T(256)S(1)}, s32[256]{0:T(256)}, u32[]{:S(2)}) copy-start(s32[256]{0:T(256)} %param.15) | copy-start | bytes 3076
  1.5 0.9 %copy-start = (f32[6,16,256]{2,1,0:T(8,128)S(1)}, f32[6,16,256]{2,1,0:T(8,128)}, u32[]{:S(2)}) copy-start(f32[6,16,256]{2,1,0:T(8,128)} %state.1) | copy-start | bytes 294916
  2.4 0.9 %copy-start.1 = (f32[6,16,256]{2,1,0:T(8,128)S(1)}, f32[6,16,256]{2,1,0:T(8,128)}, u32[]{:S(2)}) copy-start(f32[6,16,256]{2,1,0:T(8,128)} %cot.1) | copy-start | bytes 294916
  3.3 0.8 %copy-start.3 = (f32[64,64]{1,0:T(8,128)S(1)}, f32[64,64]{1,0:T(8,128)}, u32[]{:S(2)}) copy-start(f32[64,64]{1,0:T(8,128)} %rad.1) | copy-start | bytes 49156

commit v2 on v1

--- a/solution.py
+++ b/solution.py
@@ -10,6 +10,7 @@
 NF = 6
 NY = 64
 LANES = 128
+LEVEL_BITS = 4
 MESH = pl.DeviceIdType.MESH
 F32 = jnp.float32
 BF16 = jnp.bfloat16
@@ -33,12 +34,13 @@
 
 def kernel(
     nz, nx, levels, hid, share,
-    state, cot, w_in, w_mid, w_out, rad, fall, act,
+    state_hbm, cot_hbm, w_in_hbm, w_mid_hbm, w_out_hbm, rad_hbm, fall_hbm, act_hbm,
     new_state, state_grad, g_mid, g_in, g_out,
+    state, cot, w_in, w_mid, w_out, rad, fall, act, pick_in, pick_out,
     sp, lp, gp, tg, tl, dxs, dys, moved, feats, out_cot, t1s, t2s, h1s, h2s,
     k1, k1t, k2, k2t, wmt, pre1, pre2, by_in, by_out, radt, tab, fcs, acc, a_in, a_out, a_mid,
     pack, part, parts, full,
-    halo_send, halo_recv, gz_send, gz_recv, rs_send, rs_recv, ag_send, ag_recv, fin_send, fin_recv,
+    load_sem, store_sem, halo_send, halo_recv, gz_send, gz_recv, rs_send, rs_recv, ag_send, ag_recv, fin_send, fin_recv,
 ):
     mz, mx = lax.axis_index("gz"), lax.axis_index("gx")
     left, right = lax.rem(mx + nx - 1, nx), lax.rem(mx + 1, nx)
@@ -54,29 +56,50 @@
             barrier, inc=1, device_id=(mz, lax.rem(mx + o, nx)), device_id_type=MESH
         )
 
-    def spread(rows, cols):
-        return (iota((rows, cols), 1) // levels == iota((rows, cols), 0)).astype(F32).astype(BF16)
+    loads = [
+        pltpu.make_async_copy(src, dst, load_sem.at[at])
+        for at, (src, dst) in enumerate(
+            [
+                (state_hbm, state), (cot_hbm, cot), (w_in_hbm, w_in), (w_mid_hbm, w_mid),
+                (w_out_hbm, w_out), (rad_hbm, rad), (fall_hbm, fall), (act_hbm, act),
+            ]
+        )
+    ]
+    for copy in loads:
+        copy.start()
+    a_in[...] = jnp.zeros_like(a_in)
+    a_out[...] = jnp.zeros_like(a_out)
+    a_mid[...] = jnp.zeros_like(a_mid)
+    for copy in loads:
+        copy.wait()
 
     def spread_t(rows, cols):
-        return (iota((rows, cols), 0) // levels == iota((rows, cols), 1)).astype(F32).astype(BF16)
+        return (iota((rows, cols), 0) >> LEVEL_BITS == iota((rows, cols), 1)).astype(F32).astype(BF16)
 
     eye = (iota((hid, hid), 0) == iota((hid, hid), 1)).astype(F32).astype(BF16)
-    w1 = mm(w_in[...], spread(2 * NF, 2 * NF * levels))
-    w1t = mm_t(spread_t(2 * NF * levels, 2 * NF), w_in[...])
+    w1t = mm(spread_t(2 * NF * levels, 2 * NF), w_in[...])
+    w1 = mm_t(eye, w1t.astype(BF16))
     w2 = mm(spread_t(NF * levels, NF), w_out[...])
     w2t = mm_t(eye, w2.astype(BF16))
     wmt[...] = mm_t(eye, w_mid[...]).astype(BF16)
 
     def place(z, carry):
         rows = pl.ds(pl.multiple_of(z * hid, hid), hid)
-        k1[rows, :] = jnp.where(iota(w1.shape, 1) % levels == z, w1, 0.0).astype(BF16)
-        k2t[rows, :] = jnp.where(iota(w2t.shape, 1) % levels == z, w2t, 0.0).astype(BF16)
-        k1t[:, rows] = jnp.where(iota(w1t.shape, 0) % levels == z, w1t, 0.0).astype(BF16)
-        k2[:, rows] = jnp.where(iota(w2.shape, 0) % levels == z, w2, 0.0).astype(BF16)
+        k1[rows, :] = jnp.where(iota(w1.shape, 1) & (levels - 1) == z, w1, 0.0).astype(BF16)
+        k2t[rows, :] = jnp.where(iota(w2t.shape, 1) & (levels - 1) == z, w2t, 0.0).astype(BF16)
+        k1t[:, rows] = jnp.where(iota(w1t.shape, 0) & (levels - 1) == z, w1t, 0.0).astype(BF16)
+        k2[:, rows] = jnp.where(iota(w2.shape, 0) & (levels - 1) == z, w2, 0.0).astype(BF16)
         return carry
 
     lax.fori_loop(0, levels, place, 0)
     radt[...] = rad[...].T
+
+    def gathered(cols):
+        at = iota((levels * 16, cols), 0)
+        return ((at & 15) * levels + (at >> 4) == iota((levels * 16, cols), 1)).astype(F32).astype(BF16)
+
+    pick_in[...] = gathered(2 * NF * levels)
+    pick_out[...] = gathered(NF * levels)
 
     columns = 2 * LANES
     shape = (levels, columns)
@@ -89,8 +112,8 @@
     up, down = jnp.ones(shape, F32), jnp.ones(shape, F32)
     level = iota(shape, 0)
     for bit in range(5):
-        up = jnp.where(((level + 1) // (1 << bit)) % 2 == 1, up * powers[bit], up)
-        down = jnp.where(((levels - level) // (1 << bit)) % 2 == 1, down * powers[bit], down)
+        up = jnp.where(((level + 1) >> bit) & 1 == 1, up * powers[bit], up)
+        down = jnp.where(((levels - level) >> bit) & 1 == 1, down * powers[bit], down)
     for at, value in enumerate(
         powers + [1.0 / (1.0 + rate), jnp.broadcast_to(act[...].astype(F32), shape), down, up]
     ):
@@ -101,10 +124,6 @@
         sp[0, c + 1] = state[:, :, lanes]
         lp[0, c + 1] = (2.0 / 3.0) * cot[:, :, lanes]
         acc[c] = cot[:, :, lanes] / 3.0
-    a_in[...] = jnp.zeros_like(a_in)
-    a_out[...] = jnp.zeros_like(a_out)
-    a_mid[...] = jnp.zeros_like(a_mid)
-
     pl.semaphore_wait(barrier, nz - 1 + nx - 1)
 
     def halo(buf, kind, k):
@@ -143,7 +162,7 @@
 
     lane = iota((1, levels, LANES), 2)
     low = lane < NY
-    y_last, y_first = lane % NY == NY - 1, lane % NY == 0
+    y_last, y_first = lane & (NY - 1) == NY - 1, lane & (NY - 1) == 0
     depth = iota((levels, LANES), 0)
 
     def along_x(chunks):
@@ -152,7 +171,7 @@
         for i in (1, 2):
             plus = jnp.where(low, turned[i], turned[i + 1])
             minus = jnp.where(low, turned[i - 1], turned[i])
-            out.append((plus, minus, (8.0 * (plus - minus) - (chunks[i + 1] - chunks[i - 1])) / 12.0))
+            out.append((plus, minus, (8.0 * (plus - minus) - (chunks[i + 1] - chunks[i - 1])) * (1.0 / 12.0)))
         return out
 
     def along_y(chunk):
@@ -205,7 +224,7 @@
         for c in range(2):
             y_plus, y_minus = along_y(own[c])
             x_plus, x_minus, deriv_x = x_sides[c]
-            deriv_y = (y_plus - y_minus) / 2.0
+            deriv_y = (y_plus - y_minus) * 0.5
             laplace = x_plus + x_minus + y_plus + y_minus - 4.0 * own[c]
             dxs[k, c] = deriv_x
             dys[k, c] = deriv_y
@@ -218,13 +237,14 @@
             )
 
         def layers(group, inner):
+            block = pl.ds(pl.multiple_of(group * (4 * hid), 4 * hid), 4 * hid)
+            t1 = jnp.tanh(mm(k1[block, :], feats[k]))
+            t1s[k, block, :] = t1
+            h1 = t1.astype(BF16)
+            h1s[k, block, :] = h1
             for j in range(4):
                 rows = pl.ds(pl.multiple_of((group * 4 + j) * hid, hid), hid)
-                t1 = jnp.tanh(mm(k1[rows, :], feats[k]))
-                t1s[k, rows, :] = t1
-                h1 = t1.astype(BF16)
-                h1s[k, rows, :] = h1
-                t2 = jnp.tanh(mm(w_mid[...], h1))
+                t2 = jnp.tanh(mm(w_mid[...], h1[j * hid : (j + 1) * hid]))
                 t2s[k, rows, :] = t2
                 h2s[k, rows, :] = t2.astype(BF16)
             return inner
@@ -259,13 +279,27 @@
         return carry
 
     lax.fori_loop(0, 3, forward, 0)
+    stores = []
     for c in range(2):
-        new_state[:, :, chunk_lanes(c)] = sp[3, c + 1]
-
-
-    def gathered(cols):
-        at = iota((levels * 16, cols), 0)
-        return ((at % 16) * levels + at // 16 == iota((levels * 16, cols), 1)).astype(F32).astype(BF16)
+        stores.append(
+            pltpu.make_async_copy(
+                sp.at[3, c + 1], new_state.at[:, :, chunk_lanes(c)], store_sem.at[c]
+            )
+        )
+        stores[-1].start()
+
+
+    total_rows = nz * share
+    scatter = []
+    for o in range(1, nz):
+        peer = lax.rem(mz + o, nz)
+        scatter.append(
+            pltpu.make_async_remote_copy(
+                src_ref=pack.at[peer], dst_ref=part.at[o],
+                send_sem=rs_send.at[o], recv_sem=rs_recv.at[o],
+                device_id=(peer, mx), device_id_type=MESH,
+            )
+        )
 
     def backward(i, carry):
         k = 2 - i
@@ -288,13 +322,15 @@
             copy.start()
 
         def layers(group, inner):
+            block = pl.ds(pl.multiple_of(group * (4 * hid), 4 * hid), 4 * hid)
+            t2 = t2s[k, block, :]
+            p2 = (mm(k2t[block, :], out_cot[...]) * (1.0 - t2 * t2)).astype(BF16)
+            pre2[block, :] = p2
             for j in range(4):
                 rows = pl.ds(pl.multiple_of((group * 4 + j) * hid, hid), hid)
-                t2 = t2s[k, rows, :]
-                p2 = (mm(k2t[rows, :], out_cot[...]) * (1.0 - t2 * t2)).astype(BF16)
-                pre2[rows, :] = p2
                 t1 = t1s[k, rows, :]
-                pre1[rows, :] = (mm(wmt[...], p2) * (1.0 - t1 * t1)).astype(BF16)
+                back = mm(wmt[...], p2[j * hid : (j + 1) * hid])
+                pre1[rows, :] = (back * (1.0 - t1 * t1)).astype(BF16)
             return inner
 
         lax.fori_loop(0, levels // 4, layers, 0)
@@ -310,8 +346,8 @@
         for copy in rims:
             copy.start()
 
-        by_in[...] = mm(gathered(2 * NF * levels), feats[k]).astype(BF16)
-        by_out[...] = mm(gathered(NF * levels), out_cot[...]).astype(BF16)
+        by_in[...] = mm(pick_in[...], feats[k]).astype(BF16)
+        by_out[...] = mm(pick_out[...], out_cot[...]).astype(BF16)
 
         def terms(group, inner):
             s_in, s_out, s_mid = inner
@@ -330,6 +366,21 @@
         a_in[...] = s_in
         a_out[...] = s_out
         a_mid[...] = s_mid
+
+        @pl.when(k == 0)
+        def _():
+            everything = jnp.concatenate(
+                [
+                    a_mid[...],
+                    a_in[...],
+                    a_out[0:8, :],
+                    jnp.zeros((total_rows - hid - 24, LANES), F32),
+                ],
+                0,
+            )
+            pack[...] = everything.reshape(nz, share, LANES)
+            for copy in scatter:
+                copy.start()
 
         for copy in halos:
             copy.wait_recv()
@@ -353,7 +404,7 @@
             x_plus, x_minus, _ = lam_sides[c]
             carried_plus, carried_minus = along_y(sp[k, c + 1, 1:2] * now)
             back = (
-                (carried_plus - carried_minus) / 2.0
+                (carried_plus - carried_minus) * 0.5
                 - g_sides[c][2]
                 + 0.1 * (x_plus + x_minus + y_plus + y_minus - 4.0 * now)
                 + fcs[c]
@@ -379,31 +430,13 @@
 
     lax.fori_loop(0, 3, backward, 0)
     for c in range(2):
-        state_grad[:, :, chunk_lanes(c)] = acc[c]
-
-    total_rows = nz * share
-    everything = jnp.concatenate(
-        [
-            a_mid[...],
-            a_in[...],
-            a_out[0:8, :],
-            jnp.zeros((total_rows - hid - 24, LANES), F32),
-        ],
-        0,
-    )
-    pack[...] = everything.reshape(nz, share, LANES)
-    scatter = []
-    for o in range(1, nz):
-        peer = lax.rem(mz + o, nz)
-        scatter.append(
-            pltpu.make_async_remote_copy(
-                src_ref=pack.at[peer], dst_ref=part.at[o],
-                send_sem=rs_send.at[o], recv_sem=rs_recv.at[o],
-                device_id=(peer, mx), device_id_type=MESH,
-            )
-        )
-    for copy in scatter:
-        copy.start()
+        stores.append(
+            pltpu.make_async_copy(
+                acc.at[c], state_grad.at[:, :, chunk_lanes(c)], store_sem.at[2 + c]
+            )
+        )
+        stores[-1].start()
+
     mine = pack[mz]
     for o in range(1, nz):
         scatter[o - 1].wait_recv()
@@ -428,7 +461,11 @@
     summed = parts[0]
     for j in range(1, nx):
         summed = summed + parts[j]
-    full[mz] = 0.25 * summed
+
+    def quarter(index):
+        return pl.ds(pl.multiple_of(index * share, 8), share)
+
+    full[quarter(mz), :] = 0.25 * summed
 
     sends_z, receives_z = [], []
     for o in range(1, nz):
@@ -436,7 +473,7 @@
         for dst, to in ((mz, sends_z), (source, receives_z)):
             to.append(
                 pltpu.make_async_remote_copy(
-                    src_ref=full.at[mz], dst_ref=full.at[dst],
+                    src_ref=full.at[quarter(mz)], dst_ref=full.at[quarter(dst)],
                     send_sem=fin_send.at[o], recv_sem=fin_recv.at[dst],
                     device_id=(peer, mx), device_id_type=MESH,
                 )
@@ -445,12 +482,27 @@
         copy.start()
     for copy in receives_z:
         copy.wait_recv()
-    result = full[...].reshape(total_rows, LANES)
-    g_mid[...] = result[0:hid]
-    g_in[...] = result[hid : hid + 16]
-    g_out[...] = result[hid + 16 : hid + 24]
+    for at, (out, first, count) in enumerate(
+        ((g_mid, 0, hid), (g_in, hid, 2 * NF), (g_out, hid + 16, NF))
+    ):
+        stores.append(
+            pltpu.make_async_copy(full.at[first : first + count], out, store_sem.at[4 + at])
+        )
+        stores[-1].start()
+    for copy in stores:
+        copy.wait()
     for copy in scatter + sends + sends_z:
         copy.wait_send()
+
+
+def write_out(*refs):
+    copies = [
+        pltpu.make_async_copy(refs[at], refs[5 + at], refs[10].at[at]) for at in range(5)
+    ]
+    for copy in copies:
+        copy.start()
+    for copy in copies:
+        copy.wait()
 
 
 def on_device(nz, nx, state, state_cot, w_in, w_mid, w_out, radiation, fall_rate, active):
@@ -465,6 +517,16 @@
     dma = pltpu.SemaphoreType.DMA
     vmem = pltpu.VMEM
     scratch = [
+        vmem(state.shape, F32),
+        vmem(state.shape, F32),
+        vmem((2 * NF, hid), BF16),
+        vmem((hid, hid), BF16),
+        vmem((NF, hid), BF16),
+        vmem(radiation.shape, F32),
+        vmem((1, columns), F32),
+        vmem((1, columns), active.dtype),
+        vmem((levels * 16, 2 * wide), BF16),
+        vmem((levels * 16, wide), BF16),
         vmem((4,) + chunk, F32),
         vmem((4,) + chunk, F32),
         vmem((3,) + chunk, F32),
@@ -498,35 +560,44 @@
         vmem((nz, share, LANES), F32),
         vmem((nz, share, LANES), F32),
         vmem((nx, share, LANES), F32),
-        vmem((nz, share, LANES), F32),
+        vmem((nz * share, LANES), F32),
+        dma((8,)), dma((7,)),
         dma((3, 3, 2)), dma((3, 3, 2)),
         dma((2, 3, nz)), dma((2, 3, nz)),
         dma((nz,)), dma((nz,)),
         dma((nx,)), dma((nx,)),
         dma((nz,)), dma((nz,)),
     ]
-    whole = pl.BlockSpec(memory_space=pltpu.VMEM)
-    new_state, state_grad, g_mid, g_in, g_out = pl.pallas_call(
+    results = pl.pallas_call(
         functools.partial(kernel, nz, nx, levels, hid, share),
         out_shape=(
             jax.ShapeDtypeStruct(state.shape, F32),
             jax.ShapeDtypeStruct(state.shape, F32),
             jax.ShapeDtypeStruct((hid, hid), F32),
-            jax.ShapeDtypeStruct((16, hid), F32),
-            jax.ShapeDtypeStruct((8, hid), F32),
+            jax.ShapeDtypeStruct((2 * NF, hid), F32),
+            jax.ShapeDtypeStruct((NF, hid), F32),
         ),
-        in_specs=[whole] * 8,
-        out_specs=[whole] * 5,
+        in_specs=[pl.BlockSpec(memory_space=pl.ANY)] * 8,
+        out_specs=[pl.BlockSpec(memory_space=pl.ANY)] * 5,
         scratch_shapes=scratch,
         compiler_params=pltpu.CompilerParams(
-            collective_id=0, has_side_effects=True, vmem_limit_bytes=48 * 1024 * 1024
+            collective_id=0, has_side_effects=True, vmem_limit_bytes=56 * 1024 * 1024
         ),
         name="adjoint_step",
     )(
-        state, state_cot, w_in, w_mid, w_out, radiation,
+        state, state_cot, w_in.T, w_mid, w_out, radiation,
         fall_rate.reshape(1, columns), active.reshape(1, columns),
     )
-    return new_state, state_grad, g_in[: 2 * NF].T, g_mid, g_out[:NF]
+    new_state, state_grad, g_mid, g_in, g_out = pl.pallas_call(
+        write_out,
+        out_shape=tuple(jax.ShapeDtypeStruct(r.shape, r.dtype) for r in results),
+        in_specs=[pl.BlockSpec(memory_space=pl.ANY)] * 5,
+        out_specs=[pl.BlockSpec(memory_space=pl.ANY)] * 5,
+        scratch_shapes=[dma((5,))],
+        compiler_params=pltpu.CompilerParams(vmem_limit_bytes=56 * 1024 * 1024),
+        name="write_out",
+    )(*results)
+    return new_state, state_grad, g_in.T, g_mid, g_out
 
 
 def solution(mesh):

time: 67.2 us -> 67.2 us (level)
  Pallas kernels: 59.6 us -> 66.4 us
  local copies, waits for them, and re-layouts: 6.49 us -> 0 us
    pallas_call x0 -> x1, Pallas kernels: none -> 9.37 us  [on_device(): pl.pallas_call(write_out, out_shape=tuple((jax.ShapeDtypeStruct(r.shape,...]
    unnamed x19 -> x0, local copies, waits for them, and re-layouts: 5.89 us -> none
    pallas_call x1, Pallas kernels: 59.6 us -> 57 us  [on_device(): pl.pallas_call(functools.partial(kernel, nz, nx, levels, hid, share), out...]
where the time goes in v2:
time: 67.2 us; the launch traced here: 67.1 us
  Pallas kernels  66.4 us (99%)
    pallas_call x1, Pallas kernels, on_device(): pl.pallas_call(functools.partial(kernel, nz, nx, levels, hid, share), out...  57 us
    pallas_call x1, Pallas kernels, on_device(): pl.pallas_call(write_out, out_shape=tuple((jax.ShapeDtypeStruct(r.shape,...  9.37 us

profile of v2, /device:TPU:0, one launch (start us, length us, event | category | flops | bytes accessed | tf_op | source)
XLA Modules:
  0.0 67.1 jit_solution(3218218581682497025)
XLA Ops:
  0.6 57.0 %adjoint_step.1 = (f32[6,16,256]{2,1,0:T(8,128)}, f32[6,16,256]{2,1,0:T(8,128)}, f32[128,128]{1,0:T(8,128)}, f32[12,128]{1,0:T(8,128)}, f32[6,128]{1,0:T(8,128)}) custom-call(f32[6,16,256]{2,1,0:T(8,128)} %state_hbm.1, f32[6,16,256]{2,1,0:T(8,128)} %cot_hbm.1, bf16[12,128]{1,0:T(8,128)(2,1)} %bitcast.4, bf16[128,128]{1,0:T(8,128)(2,1)} %w_mid_hbm.1, ...), custom_call_target="tpu_custom_call" | custom-call | tf_op jit(solution)/shard_map/adjoint_step/pallas_call | solution.py:571
  57.7 9.4 %write_out.1 = (f32[6,16,256]{2,1,0:T(8,128)}, f32[6,16,256]{2,1,0:T(8,128)}, f32[128,128]{1,0:T(8,128)}, f32[12,128]{1,0:T(8,128)}, f32[6,128]{1,0:T(8,128)}) custom-call(f32[6,16,256]{2,1,0:T(8,128)} %get-tuple-element.15.refs_0_, f32[6,16,256]{2,1,0:T(8,128)} %get-tuple-element.16.refs_1_, f32[128,128]{1,0:T(8,128)} %get-tuple-element.17.refs_2_, ...), custom_call_target="tpu_custom_call" | custom-call | tf_op jit(solution)/shard_map/write_out/pallas_call | solution.py:591

commit v3 on v2

--- a/solution.py
+++ b/solution.py
@@ -10,7 +10,8 @@
 NF = 6
 NY = 64
 LANES = 128
-LEVEL_BITS = 4
+HALF = 8
+HALF_BITS = 3
 MESH = pl.DeviceIdType.MESH
 F32 = jnp.float32
 BF16 = jnp.bfloat16
@@ -37,14 +38,13 @@
     state_hbm, cot_hbm, w_in_hbm, w_mid_hbm, w_out_hbm, rad_hbm, fall_hbm, act_hbm,
     new_state, state_grad, g_mid, g_in, g_out,
     state, cot, w_in, w_mid, w_out, rad, fall, act, pick_in, pick_out,
-    sp, lp, gp, tg, tl, dxs, dys, moved, feats, out_cot, t1s, t2s, h1s, h2s,
+    sp, lp, gp, rim_out, rim_in, fallv, tg, tl, dxs, dys, moved, feats, out_cot, t1s, t2s, h1s, h2s,
     k1, k1t, k2, k2t, wmt, pre1, pre2, by_in, by_out, radt, tab, fcs, acc, a_in, a_out, a_mid,
     pack, part, parts, full,
     load_sem, store_sem, halo_send, halo_recv, gz_send, gz_recv, rs_send, rs_recv, ag_send, ag_recv, fin_send, fin_recv,
 ):
     mz, mx = lax.axis_index("gz"), lax.axis_index("gx")
     left, right = lax.rem(mx + nx - 1, nx), lax.rem(mx + 1, nx)
-    rows_all = levels * hid
 
     barrier = pltpu.get_barrier_semaphore()
     for o in range(1, nz):
@@ -72,34 +72,6 @@
     a_mid[...] = jnp.zeros_like(a_mid)
     for copy in loads:
         copy.wait()
-
-    def spread_t(rows, cols):
-        return (iota((rows, cols), 0) >> LEVEL_BITS == iota((rows, cols), 1)).astype(F32).astype(BF16)
-
-    eye = (iota((hid, hid), 0) == iota((hid, hid), 1)).astype(F32).astype(BF16)
-    w1t = mm(spread_t(2 * NF * levels, 2 * NF), w_in[...])
-    w1 = mm_t(eye, w1t.astype(BF16))
-    w2 = mm(spread_t(NF * levels, NF), w_out[...])
-    w2t = mm_t(eye, w2.astype(BF16))
-    wmt[...] = mm_t(eye, w_mid[...]).astype(BF16)
-
-    def place(z, carry):
-        rows = pl.ds(pl.multiple_of(z * hid, hid), hid)
-        k1[rows, :] = jnp.where(iota(w1.shape, 1) & (levels - 1) == z, w1, 0.0).astype(BF16)
-        k2t[rows, :] = jnp.where(iota(w2t.shape, 1) & (levels - 1) == z, w2t, 0.0).astype(BF16)
-        k1t[:, rows] = jnp.where(iota(w1t.shape, 0) & (levels - 1) == z, w1t, 0.0).astype(BF16)
-        k2[:, rows] = jnp.where(iota(w2.shape, 0) & (levels - 1) == z, w2, 0.0).astype(BF16)
-        return carry
-
-    lax.fori_loop(0, levels, place, 0)
-    radt[...] = rad[...].T
-
-    def gathered(cols):
-        at = iota((levels * 16, cols), 0)
-        return ((at & 15) * levels + (at >> 4) == iota((levels * 16, cols), 1)).astype(F32).astype(BF16)
-
-    pick_in[...] = gathered(2 * NF * levels)
-    pick_out[...] = gathered(NF * levels)
 
     columns = 2 * LANES
     shape = (levels, columns)
@@ -122,45 +94,50 @@
     for c in range(2):
         lanes = slice(c * LANES, (c + 1) * LANES)
         sp[0, c + 1] = state[:, :, lanes]
-        lp[0, c + 1] = (2.0 / 3.0) * cot[:, :, lanes]
-        acc[c] = cot[:, :, lanes] / 3.0
-    pl.semaphore_wait(barrier, nz - 1 + nx - 1)
-
-    def halo(buf, kind, k):
+        lp[0, c] = (2.0 / 3.0) * cot[:, :, lanes]
+        acc[c] = cot[:, :, lanes] * (1.0 / 3.0)
+
+    def rows_of(half):
+        return pl.ds(pl.multiple_of(half * HALF, HALF), HALF)
+
+    def sides(sources, targets, kind, k, half):
         return [
             pltpu.make_async_remote_copy(
-                src_ref=buf.at[k, 1], dst_ref=buf.at[k, 3],
-                send_sem=halo_send.at[kind, k, 0], recv_sem=halo_recv.at[kind, k, 0],
-                device_id=(mz, left), device_id_type=MESH,
-            ),
-            pltpu.make_async_remote_copy(
-                src_ref=buf.at[k, 2], dst_ref=buf.at[k, 0],
-                send_sem=halo_send.at[kind, k, 1], recv_sem=halo_recv.at[kind, k, 1],
-                device_id=(mz, right), device_id_type=MESH,
-            ),
+                src_ref=sources[side].at[:, rows_of(half), :],
+                dst_ref=targets[side].at[:, rows_of(half), :],
+                send_sem=halo_send.at[kind, k, half, side],
+                recv_sem=halo_recv.at[kind, k, half, side],
+                device_id=(mz, (left, right)[side]), device_id_type=MESH,
+            )
+            for side in range(2)
         ]
+
+    def halo(k, half):
+        return sides((sp.at[k, 1], sp.at[k, 2]), (sp.at[k, 3], sp.at[k, 0]), 0, k, half)
+
+    def rims(i, half):
+        return sides((rim_out.at[i, 0], rim_out.at[i, 1]), (rim_in.at[i, 1], rim_in.at[i, 0]), 1, i, half)
+
+    pl.semaphore_wait(barrier, nz - 1 + nx - 1)
+    for half in range(2):
+        for copy in halo(0, half):
+            copy.start()
 
     def level_copies(buf, kind, k):
         sends, receives = [], []
         for o in range(1, nz):
             peer, source = lax.rem(mz + o, nz), lax.rem(mz + nz - o, nz)
-            sends.append(
-                pltpu.make_async_remote_copy(
-                    src_ref=buf.at[k, mz], dst_ref=buf.at[k, mz],
-                    send_sem=gz_send.at[kind, k, o], recv_sem=gz_recv.at[kind, k, mz],
-                    device_id=(peer, mx), device_id_type=MESH,
+            for dst, to in ((mz, sends), (source, receives)):
+                to.append(
+                    pltpu.make_async_remote_copy(
+                        src_ref=buf.at[k, mz], dst_ref=buf.at[k, dst],
+                        send_sem=gz_send.at[kind, k, o], recv_sem=gz_recv.at[kind, k, dst],
+                        device_id=(peer, mx), device_id_type=MESH,
+                    )
                 )
-            )
-            receives.append(
-                pltpu.make_async_remote_copy(
-                    src_ref=buf.at[k, mz], dst_ref=buf.at[k, source],
-                    send_sem=gz_send.at[kind, k, o], recv_sem=gz_recv.at[kind, k, source],
-                    device_id=(peer, mx), device_id_type=MESH,
-                )
-            )
         return sends, receives
 
-    lane = iota((1, levels, LANES), 2)
+    lane = iota((1, 1, LANES), 2)
     low = lane < NY
     y_last, y_first = lane & (NY - 1) == NY - 1, lane & (NY - 1) == 0
     depth = iota((levels, LANES), 0)
@@ -204,57 +181,95 @@
     def chunk_lanes(c):
         return slice(c * LANES, (c + 1) * LANES)
 
-    def forward(k, carry):
-        own = [sp[k, 1], sp[k, 2]]
-        halos = halo(sp, 0, k)
-        for copy in halos:
+    def share_levels(k):
+        for c in range(2):
+            lanes = chunk_lanes(c)
+            value = settle(sp[k, c + 1, 5], lanes, True)
+            fallv[c, 0] = value
+            tg[k, mz, 0:levels, lanes] = sp[k, c + 1, 3]
+            tg[k, mz, levels:, lanes] = jnp.broadcast_to(value[0:1], (8, LANES))
+        for copy in level_copies(tg, 0, k)[0]:
             copy.start()
-        local = []
-        for c in range(2):
-            value = settle(own[c][5], chunk_lanes(c), True)
-            local.append(value)
-            tg[k, mz, 0:levels, chunk_lanes(c)] = own[c][3]
-            tg[k, mz, levels:, chunk_lanes(c)] = jnp.broadcast_to(value[0:1], (8, LANES))
-        sends, receives = level_copies(tg, 0, k)
-        for copy in sends:
-            copy.start()
-        for copy in halos:
+
+    share_levels(0)
+
+    def spread_t(rows, cols):
+        return (iota((rows, cols), 0) >> HALF_BITS == iota((rows, cols), 1)).astype(F32).astype(BF16)
+
+    eye = (iota((hid, hid), 0) == iota((hid, hid), 1)).astype(F32).astype(BF16)
+    w1t = mm(spread_t(2 * NF * HALF, 2 * NF), w_in[...])
+    w1 = mm_t(eye, w1t.astype(BF16))
+    w2 = mm(spread_t(NF * HALF, NF), w_out[...])
+    w2t = mm_t(eye, w2.astype(BF16))
+    wmt[...] = mm_t(eye, w_mid[...]).astype(BF16)
+
+    def place(z, carry):
+        rows = pl.ds(pl.multiple_of(z * hid, hid), hid)
+        k1[rows, :] = jnp.where(iota(w1.shape, 1) & (HALF - 1) == z, w1, 0.0).astype(BF16)
+        k2t[rows, :] = jnp.where(iota(w2t.shape, 1) & (HALF - 1) == z, w2t, 0.0).astype(BF16)
+        k1t[:, rows] = jnp.where(iota(w1t.shape, 0) & (HALF - 1) == z, w1t, 0.0).astype(BF16)
+        k2[:, rows] = jnp.where(iota(w2.shape, 0) & (HALF - 1) == z, w2, 0.0).astype(BF16)
+        return carry
+
+    lax.fori_loop(0, HALF, place, 0)
+    radt[...] = rad[...].T
+
+    def gathered(cols):
+        at = iota((HALF * 16, cols), 0)
+        return ((at & 15) * HALF + (at >> 4) == iota((HALF * 16, cols), 1)).astype(F32).astype(BF16)
+
+    pick_in[...] = gathered(2 * NF * HALF)
+    pick_out[...] = gathered(NF * HALF)
+
+
+    def forward(t, carry):
+        k, half = t >> 1, t & 1
+        rows8 = rows_of(half)
+        own = [sp[k, 1, :, rows8, :], sp[k, 2, :, rows8, :]]
+        for copy in halo(k, half):
             copy.wait_recv()
-        x_sides = along_x([sp[k, 0], own[0], own[1], sp[k, 3]])
+        x_sides = along_x([sp[k, 0, :, rows8, :], own[0], own[1], sp[k, 3, :, rows8, :]])
         for c in range(2):
             y_plus, y_minus = along_y(own[c])
             x_plus, x_minus, deriv_x = x_sides[c]
             deriv_y = (y_plus - y_minus) * 0.5
             laplace = x_plus + x_minus + y_plus + y_minus - 4.0 * own[c]
-            dxs[k, c] = deriv_x
-            dys[k, c] = deriv_y
+            dxs[k, c, :, rows8, :] = deriv_x
+            dys[k, c, :, rows8, :] = deriv_y
             moved[c] = -(own[c][0:1] * deriv_x + own[c][1:2] * deriv_y) + 0.1 * laplace
-            feats[k, 0 : NF * levels, chunk_lanes(c)] = (
-                own[c].reshape(NF * levels, LANES).astype(BF16)
-            )
-            feats[k, NF * levels :, chunk_lanes(c)] = (
-                deriv_x.reshape(NF * levels, LANES).astype(BF16)
+            feats[k, half, 0 : NF * HALF, chunk_lanes(c)] = (
+                own[c].reshape(NF * HALF, LANES).astype(BF16)
+            )
+            feats[k, half, NF * HALF :, chunk_lanes(c)] = (
+                deriv_x.reshape(NF * HALF, LANES).astype(BF16)
             )
 
         def layers(group, inner):
             block = pl.ds(pl.multiple_of(group * (4 * hid), 4 * hid), 4 * hid)
-            t1 = jnp.tanh(mm(k1[block, :], feats[k]))
-            t1s[k, block, :] = t1
+            first = half * (HALF * hid) + group * (4 * hid)
+            kept = pl.ds(pl.multiple_of(first, 4 * hid), 4 * hid)
+            t1 = jnp.tanh(mm(k1[block, :], feats[k, half]))
+            t1s[k, kept, :] = t1
             h1 = t1.astype(BF16)
-            h1s[k, block, :] = h1
+            h1s[k, kept, :] = h1
             for j in range(4):
-                rows = pl.ds(pl.multiple_of((group * 4 + j) * hid, hid), hid)
+                rows = pl.ds(pl.multiple_of(first + j * hid, hid), hid)
                 t2 = jnp.tanh(mm(w_mid[...], h1[j * hid : (j + 1) * hid]))
                 t2s[k, rows, :] = t2
                 h2s[k, rows, :] = t2.astype(BF16)
             return inner
 
-        lax.fori_loop(0, levels // 4, layers, 0)
-        closure = mm(k2[...], h2s[k])
-        for copy in receives:
-            copy.wait_recv()
+        lax.fori_loop(0, HALF // 4, layers, 0)
+        half_cells = pl.ds(pl.multiple_of(half * (HALF * hid), HALF * hid), HALF * hid)
+        closure = mm(k2[...], h2s[k, half_cells, :])
+
+        @pl.when(half == 0)
+        def _():
+            for copy in level_copies(tg, 0, k)[1]:
+                copy.wait_recv()
+
         heat = mm(
-            rad[pl.ds(pl.multiple_of(mz * levels, levels), levels), :],
+            rad[pl.ds(pl.multiple_of(mz * levels + half * HALF, HALF), HALF), :],
             tg[k, :, 0:levels, :].reshape(nz * levels, columns),
             lax.Precision.HIGHEST,
         )
@@ -262,23 +277,33 @@
         take = jnp.where(k == 0, 1.0, jnp.where(k == 1, 0.25, 2.0 / 3.0))
         for c in range(2):
             lanes = chunk_lanes(c)
-            total = moved[c] + closure[:, lanes].reshape(NF, levels, LANES)
-            fallen = local[c] + tab[7, :, lanes] * inflow(tg, k, lanes, True)
+            total = moved[c] + closure[:, lanes].reshape(NF, HALF, LANES)
+            fallen = fallv[c, 0, rows8, :] + tab[7, rows8, lanes] * inflow(tg, k, lanes, True)
             total = jnp.concatenate(
                 [
                     total[0:3],
                     total[3:4] + heat[:, lanes][None],
                     total[4:5],
-                    total[5:6] + (tab[6, :, lanes] * (fallen - own[c][5]))[None],
+                    total[5:6] + (tab[6, rows8, lanes] * (fallen - own[c][5]))[None],
                 ],
                 0,
             )
-            sp[k + 1, c + 1] = keep * state[:, :, lanes] + take * (own[c] + 0.25 * total)
-        for copy in halos + sends:
-            copy.wait_send()
+            sp[k + 1, c + 1, :, rows8, :] = (
+                keep * state[:, rows8, lanes] + take * (own[c] + 0.25 * total)
+            )
+
+        @pl.when(k < 2)
+        def _():
+            for copy in halo(k + 1, half):
+                copy.start()
+
+            @pl.when(half == 1)
+            def _():
+                share_levels(k + 1)
+
         return carry
 
-    lax.fori_loop(0, 3, forward, 0)
+    lax.fori_loop(0, 6, forward, 0)
     stores = []
     for c in range(2):
         stores.append(
@@ -303,10 +328,7 @@
 
     def backward(i, carry):
         k = 2 - i
-        lam = [lp[i, 1], lp[i, 2]]
-        halos = halo(lp, 1, i)
-        for copy in halos:
-            copy.start()
+        lam = [lp[i, 0], lp[i, 1]]
         local, masked = [], []
         for c in range(2):
             lanes = chunk_lanes(c)
@@ -316,38 +338,60 @@
             local.append(value)
             tl[i, mz, 0:levels, lanes] = lam[c][3]
             tl[i, mz, levels:, lanes] = jnp.broadcast_to(value[levels - 1 : levels], (8, LANES))
-            out_cot[:, lanes] = lam[c].reshape(NF * levels, LANES).astype(BF16)
+            for half in range(2):
+                out_cot[half, :, lanes] = (
+                    lam[c][:, half * HALF : (half + 1) * HALF, :]
+                    .reshape(NF * HALF, LANES).astype(BF16)
+                )
         sends, receives = level_copies(tl, 1, i)
         for copy in sends:
             copy.start()
 
-        def layers(group, inner):
-            block = pl.ds(pl.multiple_of(group * (4 * hid), 4 * hid), 4 * hid)
-            t2 = t2s[k, block, :]
-            p2 = (mm(k2t[block, :], out_cot[...]) * (1.0 - t2 * t2)).astype(BF16)
-            pre2[block, :] = p2
-            for j in range(4):
-                rows = pl.ds(pl.multiple_of((group * 4 + j) * hid, hid), hid)
-                t1 = t1s[k, rows, :]
-                back = mm(wmt[...], p2[j * hid : (j + 1) * hid])
-                pre1[rows, :] = (back * (1.0 - t1 * t1)).astype(BF16)
-            return inner
-
-        lax.fori_loop(0, levels // 4, layers, 0)
-        feature_cot = mm(k1t[...], pre1[...])
-        for c in range(2):
-            lanes = chunk_lanes(c)
-            fcs[c] = feature_cot[0 : NF * levels, lanes].reshape(NF, levels, LANES)
-            gp[i, c + 1] = (
-                feature_cot[NF * levels :, lanes].reshape(NF, levels, LANES)
-                - sp[k, c + 1, 0:1] * lp[i, c + 1]
-            )
-        rims = halo(gp, 2, i)
-        for copy in rims:
-            copy.start()
-
-        by_in[...] = mm(pick_in[...], feats[k]).astype(BF16)
-        by_out[...] = mm(pick_out[...], out_cot[...]).astype(BF16)
+        def by_half(half, outer):
+            rows8 = rows_of(half)
+
+            def layers(group, inner):
+                block = pl.ds(pl.multiple_of(group * (4 * hid), 4 * hid), 4 * hid)
+                first = half * (HALF * hid) + group * (4 * hid)
+                kept = pl.ds(pl.multiple_of(first, 4 * hid), 4 * hid)
+                t2 = t2s[k, kept, :]
+                p2 = (mm(k2t[block, :], out_cot[half]) * (1.0 - t2 * t2)).astype(BF16)
+                pre2[kept, :] = p2
+                for j in range(4):
+                    rows = pl.ds(pl.multiple_of(first + j * hid, hid), hid)
+                    t1 = t1s[k, rows, :]
+                    back = mm(wmt[...], p2[j * hid : (j + 1) * hid])
+                    pre1[rows, :] = (back * (1.0 - t1 * t1)).astype(BF16)
+                return inner
+
+            lax.fori_loop(0, HALF // 4, layers, 0)
+            half_cells = pl.ds(pl.multiple_of(half * (HALF * hid), HALF * hid), HALF * hid)
+            feature_cot = mm(k1t[...], pre1[half_cells, :])
+            for c in range(2):
+                lanes = chunk_lanes(c)
+                fcs[c, :, rows8, :] = feature_cot[0 : NF * HALF, lanes].reshape(NF, HALF, LANES)
+                now = lp[i, c, :, rows8, :]
+                source = (
+                    feature_cot[NF * HALF :, lanes].reshape(NF, HALF, LANES)
+                    - sp[k, c + 1, 0:1, rows8, :] * now
+                )
+                gp[c, :, rows8, :] = source
+                turned = pltpu.roll(source, NY, 2)
+                spread_lam = 0.1 * pltpu.roll(now, NY, 2)
+                if c == 0:
+                    near = (source - 8.0 * turned) * (1.0 / 12.0) + spread_lam
+                    rim_out[i, 0, :, rows8, :] = jnp.where(low, source * (1.0 / 12.0), near)
+                else:
+                    near = (8.0 * turned - source) * (1.0 / 12.0) + spread_lam
+                    rim_out[i, 1, :, rows8, :] = jnp.where(low, near, source * (-1.0 / 12.0))
+            for copy in rims(i, half):
+                copy.start()
+            few = pl.ds(pl.multiple_of(half * (HALF * 16), HALF * 16), HALF * 16)
+            by_in[few, :] = mm(pick_in[...], feats[k, half]).astype(BF16)
+            by_out[few, :] = mm(pick_out[...], out_cot[half]).astype(BF16)
+            return outer
+
+        lax.fori_loop(0, 2, by_half, 0)
 
         def terms(group, inner):
             s_in, s_out, s_mid = inner
@@ -382,8 +426,6 @@
             for copy in scatter:
                 copy.start()
 
-        for copy in halos:
-            copy.wait_recv()
         for copy in receives:
             copy.wait_recv()
         heat = mm(
@@ -391,10 +433,12 @@
             tl[i, :, 0:levels, :].reshape(nz * levels, columns),
             lax.Precision.HIGHEST,
         )
-        lam_sides = along_x([lp[i, 0], lam[0], lam[1], lp[i, 3]])
-        for copy in rims:
-            copy.wait_recv()
-        g_sides = along_x([gp[i, 0], gp[i, 1], gp[i, 2], gp[i, 3]])
+        zero = jnp.zeros((NF, levels, LANES), F32)
+        lam_sides = along_x([zero, lam[0], lam[1], zero])
+        g_sides = along_x([zero, gp[0], gp[1], zero])
+        for half in range(2):
+            for copy in rims(i, half):
+                copy.wait_recv()
         weight = jnp.where(k == 0, 1.0, jnp.where(k == 1, 0.0, 0.75))
         share_on = jnp.where(k == 2, 0.25, 1.0)
         for c in range(2):
@@ -408,6 +452,7 @@
                 - g_sides[c][2]
                 + 0.1 * (x_plus + x_minus + y_plus + y_minus - 4.0 * now)
                 + fcs[c]
+                + rim_in[i, c]
             )
             pulled = local[c] + tab[8, :, lanes] * inflow(tl, i, lanes, False)
             back = jnp.concatenate(
@@ -423,9 +468,7 @@
             )
             whole = now + 0.25 * back
             acc[c] = acc[c] + weight * whole
-            lp[i + 1, c + 1] = share_on * whole
-        for copy in halos + sends + rims:
-            copy.wait_send()
+            lp[i + 1, c] = share_on * whole
         return carry
 
     lax.fori_loop(0, 3, backward, 0)
@@ -491,17 +534,26 @@
         stores[-1].start()
     for copy in stores:
         copy.wait()
+    for k in range(3):
+        for half in range(2):
+            for copy in halo(k, half) + rims(k, half):
+                copy.wait_send()
+        for copy in level_copies(tg, 0, k)[0] + level_copies(tl, 1, k)[0]:
+            copy.wait_send()
     for copy in scatter + sends + sends_z:
         copy.wait_send()
 
 
 def write_out(*refs):
-    copies = [
-        pltpu.make_async_copy(refs[at], refs[5 + at], refs[10].at[at]) for at in range(5)
-    ]
-    for copy in copies:
+    sources, outs, held, sems = refs[:5], refs[5:10], refs[10:15], refs[15]
+    loads = [pltpu.make_async_copy(sources[at], held[at], sems.at[0, at]) for at in range(5)]
+    stores = [pltpu.make_async_copy(held[at], outs[at], sems.at[1, at]) for at in range(5)]
+    for copy in loads:
         copy.start()
-    for copy in copies:
+    for load, store in zip(loads, stores):
+        load.wait()
+        store.start()
+    for copy in stores:
         copy.wait()
 
 
@@ -511,7 +563,7 @@
     assert fields == NF and columns == 2 * LANES and hid == LANES and levels == 16
     share = -(-(hid + 24) // (8 * nz)) * 8
     cells = levels * hid
-    wide = NF * levels
+    wide = NF * HALF
     chunk = (4, NF, levels, LANES)
     two = (2, NF, levels, LANES)
     dma = pltpu.SemaphoreType.DMA
@@ -525,26 +577,29 @@
         vmem(radiation.shape, F32),
         vmem((1, columns), F32),
         vmem((1, columns), active.dtype),
-        vmem((levels * 16, 2 * wide), BF16),
-        vmem((levels * 16, wide), BF16),
+        vmem((HALF * 16, 2 * wide), BF16),
+        vmem((HALF * 16, wide), BF16),
         vmem((4,) + chunk, F32),
-        vmem((4,) + chunk, F32),
-        vmem((3,) + chunk, F32),
+        vmem((4,) + two, F32),
+        vmem(two, F32),
+        vmem((3,) + two, F32),
+        vmem((3,) + two, F32),
+        vmem((2, 1, levels, LANES), F32),
         vmem((3, nz, levels + 8, columns), F32),
         vmem((3, nz, levels + 8, columns), F32),
         vmem((3,) + two, F32),
         vmem((3,) + two, F32),
-        vmem(two, F32),
-        vmem((3, 2 * wide, columns), BF16),
-        vmem((wide, columns), BF16),
+        vmem((2, NF, HALF, LANES), F32),
+        vmem((3, 2, 2 * wide, columns), BF16),
+        vmem((2, wide, columns), BF16),
         vmem((3, cells, columns), F32),
         vmem((3, cells, columns), F32),
         vmem((3, cells, columns), BF16),
         vmem((3, cells, columns), BF16),
-        vmem((cells, 2 * wide), BF16),
-        vmem((2 * wide, cells), BF16),
-        vmem((wide, cells), BF16),
-        vmem((cells, wide), BF16),
+        vmem((cells // 2, 2 * wide), BF16),
+        vmem((2 * wide, cells // 2), BF16),
+        vmem((wide, cells // 2), BF16),
+        vmem((cells // 2, wide), BF16),
         vmem((hid, hid), BF16),
         vmem((cells, columns), BF16),
         vmem((cells, columns), BF16),
@@ -562,7 +617,7 @@
         vmem((nx, share, LANES), F32),
         vmem((nz * share, LANES), F32),
         dma((8,)), dma((7,)),
-        dma((3, 3, 2)), dma((3, 3, 2)),
+        dma((2, 3, 2, 2)), dma((2, 3, 2, 2)),
         dma((2, 3, nz)), dma((2, 3, nz)),
         dma((nz,)), dma((nz,)),
         dma((nx,)), dma((nx,)),
@@ -593,7 +648,7 @@
         out_shape=tuple(jax.ShapeDtypeStruct(r.shape, r.dtype) for r in results),
         in_specs=[pl.BlockSpec(memory_space=pl.ANY)] * 5,
         out_specs=[pl.BlockSpec(memory_space=pl.ANY)] * 5,
-        scratch_shapes=[dma((5,))],
+        scratch_shapes=[vmem(r.shape, r.dtype) for r in results] + [dma((2, 5))],
         compiler_params=pltpu.CompilerParams(vmem_limit_bytes=56 * 1024 * 1024),
         name="write_out",
     )(*results)

time: 67.2 us -> 56.6 us (0.84)
  Pallas kernels: 66.4 us -> 55.8 us
    pallas_call x1, Pallas kernels: 9.37 us -> 1.69 us  [on_device(): pl.pallas_call(write_out, out_shape=tuple((jax.ShapeDtypeStruct(r.shape,...]
    pallas_call x1, Pallas kernels: 57 us -> 54.1 us  [on_device(): pl.pallas_call(functools.partial(kernel, nz, nx, levels, hid, share), out...]
where the time goes in v3:
time: 56.6 us; the launch traced here: 56.5 us
  Pallas kernels  55.8 us (99%)
  between operations  0.64 us (1%)
    pallas_call x1, Pallas kernels, on_device(): pl.pallas_call(functools.partial(kernel, nz, nx, levels, hid, share), out...  54.1 us
    pallas_call x1, Pallas kernels, on_device(): pl.pallas_call(write_out, out_shape=tuple((jax.ShapeDtypeStruct(r.shape,...  1.69 us

profile of v3, /device:TPU:0, one launch (start us, length us, event | category | flops | bytes accessed | tf_op | source)
XLA Modules:
  0.0 56.5 jit_solution(14594621726166314949)
XLA Ops:
  0.6 54.1 %adjoint_step.1 = (f32[6,16,256]{2,1,0:T(8,128)}, f32[6,16,256]{2,1,0:T(8,128)}, f32[128,128]{1,0:T(8,128)}, f32[12,128]{1,0:T(8,128)}, f32[6,128]{1,0:T(8,128)}) custom-call(f32[6,16,256]{2,1,0:T(8,128)} %state_hbm.1, f32[6,16,256]{2,1,0:T(8,128)} %cot_hbm.1, bf16[12,128]{1,0:T(8,128)(2,1)} %bitcast.4, bf16[128,128]{1,0:T(8,128)(2,1)} %w_mid_hbm.1, ...), custom_call_target="tpu_custom_call" | custom-call | tf_op jit(solution)/shard_map/adjoint_step/pallas_call | solution.py:626
  54.8 1.7 %write_out.1 = (f32[6,16,256]{2,1,0:T(8,128)}, f32[6,16,256]{2,1,0:T(8,128)}, f32[128,128]{1,0:T(8,128)}, f32[12,128]{1,0:T(8,128)}, f32[6,128]{1,0:T(8,128)}) custom-call(f32[6,16,256]{2,1,0:T(8,128)} %get-tuple-element.15.refs_0_, f32[6,16,256]{2,1,0:T(8,128)} %get-tuple-element.16.refs_1_, f32[128,128]{1,0:T(8,128)} %get-tuple-element.17.refs_2_, ...), custom_call_target="tpu_custom_call" | custom-call | tf_op jit(solution)/shard_map/write_out/pallas_call | solution.py:646

commit v4 on v3

--- a/solution.py
+++ b/solution.py
@@ -37,9 +37,9 @@
     nz, nx, levels, hid, share,
     state_hbm, cot_hbm, w_in_hbm, w_mid_hbm, w_out_hbm, rad_hbm, fall_hbm, act_hbm,
     new_state, state_grad, g_mid, g_in, g_out,
-    state, cot, w_in, w_mid, w_out, rad, fall, act, pick_in, pick_out,
+    state, cot, w_in, w_mid, w_out, rad, fall, act,
     sp, lp, gp, rim_out, rim_in, fallv, tg, tl, dxs, dys, moved, feats, out_cot, t1s, t2s, h1s, h2s,
-    k1, k1t, k2, k2t, wmt, pre1, pre2, by_in, by_out, radt, tab, fcs, acc, a_in, a_out, a_mid,
+    k1, k1t, k2, k2t, wmt, pre1, pre2, radt, tab, fcs, acc, a_in, a_out, a_mid,
     pack, part, parts, full,
     load_sem, store_sem, halo_send, halo_recv, gz_send, gz_recv, rs_send, rs_recv, ag_send, ag_recv, fin_send, fin_recv,
 ):
@@ -214,14 +214,6 @@
     lax.fori_loop(0, HALF, place, 0)
     radt[...] = rad[...].T
 
-    def gathered(cols):
-        at = iota((HALF * 16, cols), 0)
-        return ((at & 15) * HALF + (at >> 4) == iota((HALF * 16, cols), 1)).astype(F32).astype(BF16)
-
-    pick_in[...] = gathered(2 * NF * HALF)
-    pick_out[...] = gathered(NF * HALF)
-
-
     def forward(t, carry):
         k, half = t >> 1, t & 1
         rows8 = rows_of(half)
@@ -325,6 +317,9 @@
                 device_id=(peer, mx), device_id_type=MESH,
             )
         )
+
+    def fold(rows, cols):
+        return (iota((rows, cols), 1) >> HALF_BITS == iota((rows, cols), 0)).astype(F32)
 
     def backward(i, carry):
         k = 2 - i
@@ -386,22 +381,27 @@
                     rim_out[i, 1, :, rows8, :] = jnp.where(low, near, source * (-1.0 / 12.0))
             for copy in rims(i, half):
                 copy.start()
-            few = pl.ds(pl.multiple_of(half * (HALF * 16), HALF * 16), HALF * 16)
-            by_in[few, :] = mm(pick_in[...], feats[k, half]).astype(BF16)
-            by_out[few, :] = mm(pick_out[...], out_cot[half]).astype(BF16)
             return outer
 
         lax.fori_loop(0, 2, by_half, 0)
 
         def terms(group, inner):
             s_in, s_out, s_mid = inner
+            half = group >> 1
+            block = pl.ds(pl.multiple_of(group * (4 * hid), 4 * hid), 4 * hid)
+            for_in = mm_t(pre1[block, :], feats[k, half])
+            for_out = mm_t(h2s[k, block, :], out_cot[half])
             for j in range(4):
-                z = group * 4 + j
-                rows = pl.ds(pl.multiple_of(z * hid, hid), hid)
-                few = pl.ds(pl.multiple_of(z * 16, 16), 16)
+                z = (group & 1) * 4 + j
+                rows = pl.ds(pl.multiple_of((group * 4 + j) * hid, hid), hid)
+                part_rows = slice(j * hid, (j + 1) * hid)
                 s_mid = s_mid + mm_t(pre2[rows, :], h1s[k, rows, :])
-                s_in = s_in + mm_t(by_in[few, :], pre1[rows, :])
-                s_out = s_out + mm_t(by_out[few, :], h2s[k, rows, :])
+                s_in = s_in + jnp.where(
+                    iota(s_in.shape, 1) & (HALF - 1) == z, for_in[part_rows], 0.0
+                )
+                s_out = s_out + jnp.where(
+                    iota(s_out.shape, 1) & (HALF - 1) == z, for_out[part_rows], 0.0
+                )
             return s_in, s_out, s_mid
 
         s_in, s_out, s_mid = lax.fori_loop(
@@ -416,8 +416,8 @@
             everything = jnp.concatenate(
                 [
                     a_mid[...],
-                    a_in[...],
-                    a_out[0:8, :],
+                    mm_t(fold(16, 2 * NF * HALF), a_in[...], lax.Precision.HIGHEST),
+                    mm_t(fold(8, NF * HALF), a_out[...], lax.Precision.HIGHEST),
                     jnp.zeros((total_rows - hid - 24, LANES), F32),
                 ],
                 0,
@@ -484,26 +484,22 @@
     for o in range(1, nz):
         scatter[o - 1].wait_recv()
         mine = mine + part[o]
-    parts[mx] = mine
-
-    sends, receives = [], []
-    for o in range(1, nx):
-        peer, source = lax.rem(mx + o, nx), lax.rem(mx + nx - o, nx)
-        for dst, to in ((mx, sends), (source, receives)):
-            to.append(
-                pltpu.make_async_remote_copy(
-                    src_ref=parts.at[mx], dst_ref=parts.at[dst],
-                    send_sem=ag_send.at[o], recv_sem=ag_recv.at[dst],
-                    device_id=(mz, peer), device_id_type=MESH,
-                )
-            )
-    for copy in sends:
-        copy.start()
-    for copy in receives:
-        copy.wait_recv()
-    summed = parts[0]
-    for j in range(1, nx):
-        summed = summed + parts[j]
+    sends = []
+    summed = mine
+    for at in range(nx.bit_length() - 1):
+        step = 1 << at
+        partner = mx + step - 2 * step * lax.rem(lax.div(mx, step), 2)
+        parts[at, 0] = summed
+        sends.append(
+            pltpu.make_async_remote_copy(
+                src_ref=parts.at[at, 0], dst_ref=parts.at[at, 1],
+                send_sem=ag_send.at[at], recv_sem=ag_recv.at[at],
+                device_id=(mz, partner), device_id_type=MESH,
+            )
+        )
+        sends[-1].start()
+        sends[-1].wait_recv()
+        summed = summed + parts[at, 1]
 
     def quarter(index):
         return pl.ds(pl.multiple_of(index * share, 8), share)
@@ -561,6 +557,7 @@
     fields, levels, columns = state.shape
     hid = w_in.shape[0]
     assert fields == NF and columns == 2 * LANES and hid == LANES and levels == 16
+    assert nx & (nx - 1) == 0
     share = -(-(hid + 24) // (8 * nz)) * 8
     cells = levels * hid
     wide = NF * HALF
@@ -577,8 +574,6 @@
         vmem(radiation.shape, F32),
         vmem((1, columns), F32),
         vmem((1, columns), active.dtype),
-        vmem((HALF * 16, 2 * wide), BF16),
-        vmem((HALF * 16, wide), BF16),
         vmem((4,) + chunk, F32),
         vmem((4,) + two, F32),
         vmem(two, F32),
@@ -603,18 +598,16 @@
         vmem((hid, hid), BF16),
         vmem((cells, columns), BF16),
         vmem((cells, columns), BF16),
-        vmem((levels * 16, columns), BF16),
-        vmem((levels * 16, columns), BF16),
         vmem(radiation.shape, F32),
         vmem((9, levels, columns), F32),
         vmem(two, F32),
         vmem(two, F32),
-        vmem((16, hid), F32),
-        vmem((16, hid), F32),
+        vmem((hid, 2 * wide), F32),
+        vmem((hid, wide), F32),
         vmem((hid, hid), F32),
         vmem((nz, share, LANES), F32),
         vmem((nz, share, LANES), F32),
-        vmem((nx, share, LANES), F32),
+        vmem((nx.bit_length() - 1, 2, share, LANES), F32),
         vmem((nz * share, LANES), F32),
         dma((8,)), dma((7,)),
         dma((2, 3, 2, 2)), dma((2, 3, 2, 2)),

time: 56.6 us -> 60.6 us (1.071)
  Pallas kernels: 55.8 us -> 59.8 us
    pallas_call x1, Pallas kernels: 54.1 us -> 58.1 us  [on_device(): pl.pallas_call(functools.partial(kernel, nz, nx, levels, hid, share), out...]
where the time goes in v4:
time: 60.6 us; the launch traced here: 60.4 us
  Pallas kernels  59.8 us (99%)
  between operations  0.64 us (1%)
    pallas_call x1, Pallas kernels, on_device(): pl.pallas_call(functools.partial(kernel, nz, nx, levels, hid, share), out...  58.1 us
    pallas_call x1, Pallas kernels, on_device(): pl.pallas_call(write_out, out_shape=tuple((jax.ShapeDtypeStruct(r.shape,...  1.69 us

profile of v4, /device:TPU:0, one launch (start us, length us, event | category | flops | bytes accessed | tf_op | source)
XLA Modules:
  0.0 60.4 jit_solution(2311099888181991653)
XLA Ops:
  0.6 58.1 %adjoint_step.1 = (f32[6,16,256]{2,1,0:T(8,128)}, f32[6,16,256]{2,1,0:T(8,128)}, f32[128,128]{1,0:T(8,128)}, f32[12,128]{1,0:T(8,128)}, f32[6,128]{1,0:T(8,128)}) custom-call(f32[6,16,256]{2,1,0:T(8,128)} %state_hbm.1, f32[6,16,256]{2,1,0:T(8,128)} %cot_hbm.1, bf16[12,128]{1,0:T(8,128)(2,1)} %bitcast.4, bf16[128,128]{1,0:T(8,128)(2,1)} %w_mid_hbm.1, ...), custom_call_target="tpu_custom_call" | custom-call | tf_op jit(solution)/shard_map/adjoint_step/pallas_call | solution.py:619
  58.7 1.7 %write_out.1 = (f32[6,16,256]{2,1,0:T(8,128)}, f32[6,16,256]{2,1,0:T(8,128)}, f32[128,128]{1,0:T(8,128)}, f32[12,128]{1,0:T(8,128)}, f32[6,128]{1,0:T(8,128)}) custom-call(f32[6,16,256]{2,1,0:T(8,128)} %get-tuple-element.15.refs_0_, f32[6,16,256]{2,1,0:T(8,128)} %get-tuple-element.16.refs_1_, f32[128,128]{1,0:T(8,128)} %get-tuple-element.17.refs_2_, ...), custom_call_target="tpu_custom_call" | custom-call | tf_op jit(solution)/shard_map/write_out/pallas_call | solution.py:639

commit v5 on v3

--- a/solution.py
+++ b/solution.py
@@ -248,15 +248,16 @@
             block = pl.ds(pl.multiple_of(group * (4 * hid), 4 * hid), 4 * hid)
             first = half * (HALF * hid) + group * (4 * hid)
             kept = pl.ds(pl.multiple_of(first, 4 * hid), 4 * hid)
+            middle = w_mid[...]
             t1 = jnp.tanh(mm(k1[block, :], feats[k, half]))
+            h1 = t1.astype(BF16)
+            t2 = [jnp.tanh(mm(middle, h1[j * hid : (j + 1) * hid])) for j in range(4)]
             t1s[k, kept, :] = t1
-            h1 = t1.astype(BF16)
             h1s[k, kept, :] = h1
             for j in range(4):
                 rows = pl.ds(pl.multiple_of(first + j * hid, hid), hid)
-                t2 = jnp.tanh(mm(w_mid[...], h1[j * hid : (j + 1) * hid]))
-                t2s[k, rows, :] = t2
-                h2s[k, rows, :] = t2.astype(BF16)
+                t2s[k, rows, :] = t2[j]
+                h2s[k, rows, :] = t2[j].astype(BF16)
             return inner
 
         lax.fori_loop(0, HALF // 4, layers, 0)
@@ -355,13 +356,18 @@
                 first = half * (HALF * hid) + group * (4 * hid)
                 kept = pl.ds(pl.multiple_of(first, 4 * hid), 4 * hid)
                 t2 = t2s[k, kept, :]
+                t1 = t1s[k, kept, :]
+                middle = wmt[...]
                 p2 = (mm(k2t[block, :], out_cot[half]) * (1.0 - t2 * t2)).astype(BF16)
+                p1 = []
+                for j in range(4):
+                    part_rows = slice(j * hid, (j + 1) * hid)
+                    back = mm(middle, p2[part_rows])
+                    p1.append((back * (1.0 - t1[part_rows] * t1[part_rows])).astype(BF16))
                 pre2[kept, :] = p2
                 for j in range(4):
                     rows = pl.ds(pl.multiple_of(first + j * hid, hid), hid)
-                    t1 = t1s[k, rows, :]
-                    back = mm(wmt[...], p2[j * hid : (j + 1) * hid])
-                    pre1[rows, :] = (back * (1.0 - t1 * t1)).astype(BF16)
+                    pre1[rows, :] = p1[j]
                 return inner
 
             lax.fori_loop(0, HALF // 4, layers, 0)

time: 56.6 us -> 56.6 us (level)
  no operation moved by 1% of the time
where the time goes in v5:
time: 56.6 us; the launch traced here: 56.5 us
  Pallas kernels  55.8 us (99%)
  between operations  0.64 us (1%)
    pallas_call x1, Pallas kernels, on_device(): pl.pallas_call(functools.partial(kernel, nz, nx, levels, hid, share), out...  54.1 us
    pallas_call x1, Pallas kernels, on_device(): pl.pallas_call(write_out, out_shape=tuple((jax.ShapeDtypeStruct(r.shape,...  1.69 us

profile of v5, /device:TPU:0, one launch (start us, length us, event | category | flops | bytes accessed | tf_op | source)
XLA Modules:
  0.0 56.5 jit_solution(3312525542525153525)
XLA Ops:
  0.6 54.1 %adjoint_step.1 = (f32[6,16,256]{2,1,0:T(8,128)}, f32[6,16,256]{2,1,0:T(8,128)}, f32[128,128]{1,0:T(8,128)}, f32[12,128]{1,0:T(8,128)}, f32[6,128]{1,0:T(8,128)}) custom-call(f32[6,16,256]{2,1,0:T(8,128)} %state_hbm.1, f32[6,16,256]{2,1,0:T(8,128)} %cot_hbm.1, bf16[12,128]{1,0:T(8,128)(2,1)} %bitcast.4, bf16[128,128]{1,0:T(8,128)(2,1)} %w_mid_hbm.1, ...), custom_call_target="tpu_custom_call" | custom-call | tf_op jit(solution)/shard_map/adjoint_step/pallas_call | solution.py:632
  54.8 1.7 %write_out.1 = (f32[6,16,256]{2,1,0:T(8,128)}, f32[6,16,256]{2,1,0:T(8,128)}, f32[128,128]{1,0:T(8,128)}, f32[12,128]{1,0:T(8,128)}, f32[6,128]{1,0:T(8,128)}) custom-call(f32[6,16,256]{2,1,0:T(8,128)} %get-tuple-element.15.refs_0_, f32[6,16,256]{2,1,0:T(8,128)} %get-tuple-element.16.refs_1_, f32[128,128]{1,0:T(8,128)} %get-tuple-element.17.refs_2_, ...), custom_call_target="tpu_custom_call" | custom-call | tf_op jit(solution)/shard_map/write_out/pallas_call | solution.py:652

commit v6 on v5

--- a/solution.py
+++ b/solution.py
@@ -38,7 +38,7 @@
     state_hbm, cot_hbm, w_in_hbm, w_mid_hbm, w_out_hbm, rad_hbm, fall_hbm, act_hbm,
     new_state, state_grad, g_mid, g_in, g_out,
     state, cot, w_in, w_mid, w_out, rad, fall, act, pick_in, pick_out,
-    sp, lp, gp, rim_out, rim_in, fallv, tg, tl, dxs, dys, moved, feats, out_cot, t1s, t2s, h1s, h2s,
+    sp, lp, gp, rim_out, rim_in, fallv, heats, tg, tl, dxs, dys, moved, feats, out_cot, t1s, t2s, h1s, h2s,
     k1, k1t, k2, k2t, wmt, pre1, pre2, by_in, by_out, radt, tab, fcs, acc, a_in, a_out, a_mid,
     pack, part, parts, full,
     load_sem, store_sem, halo_send, halo_recv, gz_send, gz_recv, rs_send, rs_recv, ag_send, ag_recv, fin_send, fin_recv,
@@ -226,41 +226,47 @@
         k, half = t >> 1, t & 1
         rows8 = rows_of(half)
         own = [sp[k, 1, :, rows8, :], sp[k, 2, :, rows8, :]]
+        y_sides = [along_y(chunk) for chunk in own]
+        carried, spread_y = [], []
+        for c in range(2):
+            y_plus, y_minus = y_sides[c]
+            deriv_y = (y_plus - y_minus) * 0.5
+            dys[k, c, :, rows8, :] = deriv_y
+            carried.append(own[c][1:2] * deriv_y)
+            spread_y.append(y_plus + y_minus - 4.0 * own[c])
+            feats[k, half, 0 : NF * HALF, chunk_lanes(c)] = (
+                own[c].reshape(NF * HALF, LANES).astype(BF16)
+            )
         for copy in halo(k, half):
             copy.wait_recv()
         x_sides = along_x([sp[k, 0, :, rows8, :], own[0], own[1], sp[k, 3, :, rows8, :]])
         for c in range(2):
-            y_plus, y_minus = along_y(own[c])
             x_plus, x_minus, deriv_x = x_sides[c]
-            deriv_y = (y_plus - y_minus) * 0.5
-            laplace = x_plus + x_minus + y_plus + y_minus - 4.0 * own[c]
             dxs[k, c, :, rows8, :] = deriv_x
-            dys[k, c, :, rows8, :] = deriv_y
-            moved[c] = -(own[c][0:1] * deriv_x + own[c][1:2] * deriv_y) + 0.1 * laplace
-            feats[k, half, 0 : NF * HALF, chunk_lanes(c)] = (
-                own[c].reshape(NF * HALF, LANES).astype(BF16)
+            moved[c] = -(own[c][0:1] * deriv_x + carried[c]) + 0.1 * (
+                x_plus + x_minus + spread_y[c]
             )
             feats[k, half, NF * HALF :, chunk_lanes(c)] = (
                 deriv_x.reshape(NF * HALF, LANES).astype(BF16)
             )
 
         def layers(group, inner):
-            block = pl.ds(pl.multiple_of(group * (4 * hid), 4 * hid), 4 * hid)
-            first = half * (HALF * hid) + group * (4 * hid)
-            kept = pl.ds(pl.multiple_of(first, 4 * hid), 4 * hid)
+            block = pl.ds(pl.multiple_of(group * (HALF * hid), HALF * hid), HALF * hid)
+            first = half * (HALF * hid) + group * (HALF * hid)
+            kept = pl.ds(pl.multiple_of(first, HALF * hid), HALF * hid)
             middle = w_mid[...]
             t1 = jnp.tanh(mm(k1[block, :], feats[k, half]))
             h1 = t1.astype(BF16)
-            t2 = [jnp.tanh(mm(middle, h1[j * hid : (j + 1) * hid])) for j in range(4)]
+            t2 = [jnp.tanh(mm(middle, h1[j * hid : (j + 1) * hid])) for j in range(HALF)]
             t1s[k, kept, :] = t1
             h1s[k, kept, :] = h1
-            for j in range(4):
+            for j in range(HALF):
                 rows = pl.ds(pl.multiple_of(first + j * hid, hid), hid)
                 t2s[k, rows, :] = t2[j]
                 h2s[k, rows, :] = t2[j].astype(BF16)
             return inner
 
-        lax.fori_loop(0, HALF // 4, layers, 0)
+        layers(0, 0)
         half_cells = pl.ds(pl.multiple_of(half * (HALF * hid), HALF * hid), HALF * hid)
         closure = mm(k2[...], h2s[k, half_cells, :])
 
@@ -268,22 +274,25 @@
         def _():
             for copy in level_copies(tg, 0, k)[1]:
                 copy.wait_recv()
-
-        heat = mm(
-            rad[pl.ds(pl.multiple_of(mz * levels + half * HALF, HALF), HALF), :],
-            tg[k, :, 0:levels, :].reshape(nz * levels, columns),
-            lax.Precision.HIGHEST,
-        )
+            heats[...] = mm(
+                rad[pl.ds(pl.multiple_of(mz * levels, levels), levels), :],
+                tg[k, :, 0:levels, :].reshape(nz * levels, columns),
+                lax.Precision.HIGHEST,
+            )
+            for c in range(2):
+                lanes = chunk_lanes(c)
+                fallv[c, 0] = fallv[c, 0] + tab[7, :, lanes] * inflow(tg, k, lanes, True)
+
         keep = jnp.where(k == 0, 0.0, jnp.where(k == 1, 0.75, 1.0 / 3.0))
         take = jnp.where(k == 0, 1.0, jnp.where(k == 1, 0.25, 2.0 / 3.0))
         for c in range(2):
             lanes = chunk_lanes(c)
             total = moved[c] + closure[:, lanes].reshape(NF, HALF, LANES)
-            fallen = fallv[c, 0, rows8, :] + tab[7, rows8, lanes] * inflow(tg, k, lanes, True)
+            fallen = fallv[c, 0, rows8, :]
             total = jnp.concatenate(
                 [
                     total[0:3],
-                    total[3:4] + heat[:, lanes][None],
+                    total[3:4] + heats[rows8, lanes][None],
                     total[4:5],
                     total[5:6] + (tab[6, rows8, lanes] * (fallen - own[c][5]))[None],
                 ],
@@ -326,6 +335,18 @@
                 device_id=(peer, mx), device_id_type=MESH,
             )
         )
+
+    sends_x, receives_x = [], []
+    for o in range(1, nx):
+        peer, source = lax.rem(mx + o, nx), lax.rem(mx + nx - o, nx)
+        for dst, to in ((mx, sends_x), (source, receives_x)):
+            to.append(
+                pltpu.make_async_remote_copy(
+                    src_ref=parts.at[mx], dst_ref=parts.at[dst],
+                    send_sem=ag_send.at[o], recv_sem=ag_recv.at[dst],
+                    device_id=(mz, peer), device_id_type=MESH,
+                )
+            )
 
     def backward(i, carry):
         k = 2 - i
@@ -352,25 +373,25 @@
             rows8 = rows_of(half)
 
             def layers(group, inner):
-                block = pl.ds(pl.multiple_of(group * (4 * hid), 4 * hid), 4 * hid)
-                first = half * (HALF * hid) + group * (4 * hid)
-                kept = pl.ds(pl.multiple_of(first, 4 * hid), 4 * hid)
+                block = pl.ds(pl.multiple_of(group * (HALF * hid), HALF * hid), HALF * hid)
+                first = half * (HALF * hid) + group * (HALF * hid)
+                kept = pl.ds(pl.multiple_of(first, HALF * hid), HALF * hid)
                 t2 = t2s[k, kept, :]
                 t1 = t1s[k, kept, :]
                 middle = wmt[...]
                 p2 = (mm(k2t[block, :], out_cot[half]) * (1.0 - t2 * t2)).astype(BF16)
                 p1 = []
-                for j in range(4):
+                for j in range(HALF):
                     part_rows = slice(j * hid, (j + 1) * hid)
                     back = mm(middle, p2[part_rows])
                     p1.append((back * (1.0 - t1[part_rows] * t1[part_rows])).astype(BF16))
                 pre2[kept, :] = p2
-                for j in range(4):
+                for j in range(HALF):
                     rows = pl.ds(pl.multiple_of(first + j * hid, hid), hid)
                     pre1[rows, :] = p1[j]
                 return inner
 
-            lax.fori_loop(0, HALF // 4, layers, 0)
+            layers(0, 0)
             half_cells = pl.ds(pl.multiple_of(half * (HALF * hid), HALF * hid), HALF * hid)
             feature_cot = mm(k1t[...], pre1[half_cells, :])
             for c in range(2):
@@ -442,11 +463,9 @@
         zero = jnp.zeros((NF, levels, LANES), F32)
         lam_sides = along_x([zero, lam[0], lam[1], zero])
         g_sides = along_x([zero, gp[0], gp[1], zero])
-        for half in range(2):
-            for copy in rims(i, half):
-                copy.wait_recv()
         weight = jnp.where(k == 0, 1.0, jnp.where(k == 1, 0.0, 0.75))
         share_on = jnp.where(k == 2, 0.25, 1.0)
+        wholes = []
         for c in range(2):
             lanes = chunk_lanes(c)
             now = lam[c]
@@ -458,7 +477,6 @@
                 - g_sides[c][2]
                 + 0.1 * (x_plus + x_minus + y_plus + y_minus - 4.0 * now)
                 + fcs[c]
-                + rim_in[i, c]
             )
             pulled = local[c] + tab[8, :, lanes] * inflow(tl, i, lanes, False)
             back = jnp.concatenate(
@@ -472,7 +490,23 @@
                 ],
                 0,
             )
-            whole = now + 0.25 * back
+            wholes.append(now + 0.25 * back)
+
+        @pl.when(k == 0)
+        def _():
+            mine = pack[mz]
+            for o in range(1, nz):
+                scatter[o - 1].wait_recv()
+                mine = mine + part[o]
+            parts[mx] = mine
+            for copy in sends_x:
+                copy.start()
+
+        for half in range(2):
+            for copy in rims(i, half):
+                copy.wait_recv()
+        for c in range(2):
+            whole = wholes[c] + 0.25 * rim_in[i, c]
             acc[c] = acc[c] + weight * whole
             lp[i + 1, c] = share_on * whole
         return carry
@@ -486,26 +520,7 @@
         )
         stores[-1].start()
 
-    mine = pack[mz]
-    for o in range(1, nz):
-        scatter[o - 1].wait_recv()
-        mine = mine + part[o]
-    parts[mx] = mine
-
-    sends, receives = [], []
-    for o in range(1, nx):
-        peer, source = lax.rem(mx + o, nx), lax.rem(mx + nx - o, nx)
-        for dst, to in ((mx, sends), (source, receives)):
-            to.append(
-                pltpu.make_async_remote_copy(
-                    src_ref=parts.at[mx], dst_ref=parts.at[dst],
-                    send_sem=ag_send.at[o], recv_sem=ag_recv.at[dst],
-                    device_id=(mz, peer), device_id_type=MESH,
-                )
-            )
-    for copy in sends:
-        copy.start()
-    for copy in receives:
+    for copy in receives_x:
         copy.wait_recv()
     summed = parts[0]
     for j in range(1, nx):
@@ -546,7 +561,7 @@
                 copy.wait_send()
         for copy in level_copies(tg, 0, k)[0] + level_copies(tl, 1, k)[0]:
             copy.wait_send()
-    for copy in scatter + sends + sends_z:
+    for copy in scatter + sends_x + sends_z:
         copy.wait_send()
 
 
@@ -591,6 +606,7 @@
         vmem((3,) + two, F32),
         vmem((3,) + two, F32),
         vmem((2, 1, levels, LANES), F32),
+        vmem((levels, columns), F32),
         vmem((3, nz, levels + 8, columns), F32),
         vmem((3, nz, levels + 8, columns), F32),
         vmem((3,) + two, F32),

time: 56.6 us -> 53.5 us (0.945)
  Pallas kernels: 55.8 us -> 52.7 us
    pallas_call x1, Pallas kernels: 54.1 us -> 51 us  [on_device(): pl.pallas_call(functools.partial(kernel, nz, nx, levels, hid, share), out...]
where the time goes in v6:
time: 53.5 us; the launch traced here: 53.3 us
  Pallas kernels  52.7 us (99%)
  between operations  0.64 us (1%)
    pallas_call x1, Pallas kernels, on_device(): pl.pallas_call(functools.partial(kernel, nz, nx, levels, hid, share), out...  51 us
    pallas_call x1, Pallas kernels, on_device(): pl.pallas_call(write_out, out_shape=tuple((jax.ShapeDtypeStruct(r.shape,...  1.69 us

profile of v6, /device:TPU:0, one launch (start us, length us, event | category | flops | bytes accessed | tf_op | source)
XLA Modules:
  0.0 53.3 jit_solution(11188058150804033511)
XLA Ops:
  0.6 51.0 %adjoint_step.1 = (f32[6,16,256]{2,1,0:T(8,128)}, f32[6,16,256]{2,1,0:T(8,128)}, f32[128,128]{1,0:T(8,128)}, f32[12,128]{1,0:T(8,128)}, f32[6,128]{1,0:T(8,128)}) custom-call(f32[6,16,256]{2,1,0:T(8,128)} %state_hbm.1, f32[6,16,256]{2,1,0:T(8,128)} %cot_hbm.1, bf16[12,128]{1,0:T(8,128)(2,1)} %bitcast.4, bf16[128,128]{1,0:T(8,128)(2,1)} %w_mid_hbm.1, ...), custom_call_target="tpu_custom_call" | custom-call | tf_op jit(solution)/shard_map/adjoint_step/pallas_call | solution.py:648
  51.7 1.7 %write_out.1 = (f32[6,16,256]{2,1,0:T(8,128)}, f32[6,16,256]{2,1,0:T(8,128)}, f32[128,128]{1,0:T(8,128)}, f32[12,128]{1,0:T(8,128)}, f32[6,128]{1,0:T(8,128)}) custom-call(f32[6,16,256]{2,1,0:T(8,128)} %get-tuple-element.15.refs_0_, f32[6,16,256]{2,1,0:T(8,128)} %get-tuple-element.16.refs_1_, f32[128,128]{1,0:T(8,128)} %get-tuple-element.17.refs_2_, ...), custom_call_target="tpu_custom_call" | custom-call | tf_op jit(solution)/shard_map/write_out/pallas_call | solution.py:668

commit v7 on v6

--- a/solution.py
+++ b/solution.py
@@ -422,8 +422,8 @@
 
         def terms(group, inner):
             s_in, s_out, s_mid = inner
-            for j in range(4):
-                z = group * 4 + j
+            for j in range(HALF):
+                z = group * HALF + j
                 rows = pl.ds(pl.multiple_of(z * hid, hid), hid)
                 few = pl.ds(pl.multiple_of(z * 16, 16), 16)
                 s_mid = s_mid + mm_t(pre2[rows, :], h1s[k, rows, :])
@@ -432,7 +432,7 @@
             return s_in, s_out, s_mid
 
         s_in, s_out, s_mid = lax.fori_loop(
-            0, levels // 4, terms, (a_in[...], a_out[...], a_mid[...])
+            0, levels // HALF, terms, (a_in[...], a_out[...], a_mid[...])
         )
         a_in[...] = s_in
         a_out[...] = s_out

time: 53.5 us -> 53.3 us (level)
  no operation moved by 1% of the time
where the time goes in v7:
time: 53.3 us; the launch traced here: 53.1 us
  Pallas kernels  52.4 us (98%)
  between operations  0.64 us (1%)
    pallas_call x1, Pallas kernels, on_device(): pl.pallas_call(functools.partial(kernel, nz, nx, levels, hid, share), out...  50.7 us
    pallas_call x1, Pallas kernels, on_device(): pl.pallas_call(write_out, out_shape=tuple((jax.ShapeDtypeStruct(r.shape,...  1.69 us

profile of v7, /device:TPU:0, one launch (start us, length us, event | category | flops | bytes accessed | tf_op | source)
XLA Modules:
  0.0 53.1 jit_solution(16187802829799387589)
XLA Ops:
  0.6 50.7 %adjoint_step.1 = (f32[6,16,256]{2,1,0:T(8,128)}, f32[6,16,256]{2,1,0:T(8,128)}, f32[128,128]{1,0:T(8,128)}, f32[12,128]{1,0:T(8,128)}, f32[6,128]{1,0:T(8,128)}) custom-call(f32[6,16,256]{2,1,0:T(8,128)} %state_hbm.1, f32[6,16,256]{2,1,0:T(8,128)} %cot_hbm.1, bf16[12,128]{1,0:T(8,128)(2,1)} %bitcast.4, bf16[128,128]{1,0:T(8,128)(2,1)} %w_mid_hbm.1, ...), custom_call_target="tpu_custom_call" | custom-call | tf_op jit(solution)/shard_map/adjoint_step/pallas_call | solution.py:648
  51.4 1.7 %write_out.1 = (f32[6,16,256]{2,1,0:T(8,128)}, f32[6,16,256]{2,1,0:T(8,128)}, f32[128,128]{1,0:T(8,128)}, f32[12,128]{1,0:T(8,128)}, f32[6,128]{1,0:T(8,128)}) custom-call(f32[6,16,256]{2,1,0:T(8,128)} %get-tuple-element.15.refs_0_, f32[6,16,256]{2,1,0:T(8,128)} %get-tuple-element.16.refs_1_, f32[128,128]{1,0:T(8,128)} %get-tuple-element.17.refs_2_, ...), custom_call_target="tpu_custom_call" | custom-call | tf_op jit(solution)/shard_map/write_out/pallas_call | solution.py:668
